TPU v7x, 32 devices: a whole 2x2x4 slice. The times are simulated.
32 devices in a mesh: row: 8 (over z, x), col: 4 (over y, core).
Axes of the slice: x: 2, y: 2, z: 4, core: 2. Of those that a mesh axis runs over, the one named last changes fastest.
Arguments:
- panel: float32 [131072, 512], P('row', 'col'), may hold values from -6 to 6
- signs: int32 [131072], P('row'), may hold values from -1 to 1, as said below
- samples: int32 [32768], replicated, may hold values from 0 to 131071, as said below
Outputs:
- sketch: float32 [32768, 512], P('row', 'col')
- gram: float32 [512, 512], P('col')
Inputs may be any that keep to these rules, and one draw needn't show every extreme that they name: `signs`: each entry is -1 or +1. `samples`: row indices, repeats allowed, unevenly spread over the row shards; in each aligned block of 4096 entries, at most 1024 entries share the value of (index % 16384) // 2048, and in every such block some value is shared by exactly 1024.
All inputs are finite; a program needn't handle non-finite values.
Results may differ from a plain program's by a relative error of at most 0.0001.
Values sent between devices are 32-bit elements; how exact they have to be, the bound alone decides.
A program may use at most 128 MiB of HBM per device.

v0:
```python
import math

import jax
import jax.numpy as jnp
from jax import lax
from jax.sharding import PartitionSpec as P


def parity(value):
    value = value ^ value >> 16
    value = value ^ value >> 8
    value = value ^ value >> 4
    value = value ^ value >> 2
    value = value ^ value >> 1
    return value & 1


def sylvester(order):
    index = jnp.arange(order, dtype=jnp.int32)
    bits = parity(index[:, None] & index[None, :])
    return (1 - 2 * bits).astype(jnp.float32)


def shards(panel, signs, samples):
    row_count, col_width = panel.shape
    device_count = lax.axis_size("row")
    my_index = lax.axis_index("row")
    inner_len = min(row_count, 256)
    outer_len = row_count // inner_len
    scale = 1.0 / math.sqrt(float(row_count * device_count))
    signed = panel * signs[:, None].astype(jnp.float32)
    shaped = signed.reshape(outer_len, inner_len, col_width)
    shaped = jnp.einsum(
        "cj,ajp->acp", sylvester(inner_len), shaped, precision=lax.Precision.HIGHEST
    )
    shaped = jnp.einsum(
        "ba,acp->bcp", sylvester(outer_len), shaped, precision=lax.Precision.HIGHEST
    )
    local_rows = shaped.reshape(row_count, col_width) * scale
    sample_total = samples.shape[0]
    slots_dev = sample_total // device_count
    owner_device = samples // row_count
    owner_local = samples % row_count
    block_len = row_count // device_count
    capacity = max(2, 2 * slots_dev // device_count)
    pieces = local_rows.reshape(device_count, block_len, col_width)
    received = lax.all_to_all(pieces, "row", split_axis=0, concat_axis=0, tiled=True)
    combined = jnp.einsum(
        "ed,dkp->ekp", sylvester(device_count), received, precision=lax.Precision.HIGHEST
    )
    combined = combined.reshape(device_count * block_len, col_width)
    owners = (owner_local // block_len).reshape(device_count, slots_dev)
    mine = owners == my_index
    rank = jnp.cumsum(mine.astype(jnp.int32), axis=1) - 1
    target = jnp.where(mine, rank, capacity)
    dest_ids = jnp.broadcast_to(
        jnp.arange(device_count, dtype=jnp.int32)[:, None], (device_count, slots_dev)
    )
    slot_ids = jnp.broadcast_to(
        jnp.arange(slots_dev, dtype=jnp.int32)[None, :], (device_count, slots_dev)
    )
    table = (
        jnp.zeros((device_count, capacity), jnp.int32)
        .at[dest_ids, target]
        .set(slot_ids, mode="drop")
    )
    filled = (
        jnp.zeros((device_count, capacity), jnp.bool_).at[dest_ids, target].set(True, mode="drop")
    )
    flat_rows = (owner_device * block_len + owner_local % block_len).reshape(
        device_count, slots_dev
    )
    pick_index = jnp.take_along_axis(flat_rows, table, axis=1)
    outgoing = jnp.take(combined, pick_index.reshape(-1), axis=0).reshape(
        device_count, capacity, col_width
    )
    outgoing = jnp.where(filled[:, :, None], outgoing, jnp.float32(0.0))
    arrived = lax.all_to_all(outgoing, "row", split_axis=0, concat_axis=0, tiled=True)
    my_owners = lax.dynamic_slice_in_dim(owner_local, my_index * slots_dev, slots_dev) // block_len
    onehot = (my_owners[:, None] == jnp.arange(device_count, dtype=jnp.int32)[None, :]).astype(
        jnp.int32
    )
    ranks = jnp.cumsum(onehot, axis=0) - 1
    position = jnp.take_along_axis(ranks, my_owners[:, None], axis=1)[:, 0]
    sketch = jnp.take(
        arrived.reshape(device_count * capacity, col_width), my_owners * capacity + position, axis=0
    )
    every_panel = lax.all_gather(sketch, "col", axis=1, tiled=True)
    partial_gram = jnp.dot(
        sketch.T, every_panel, precision=lax.Precision.HIGHEST, preferred_element_type=jnp.float32
    )
    gram = lax.psum(partial_gram, "row") / sample_total
    return (sketch, gram)


def solution(mesh):
    return jax.shard_map(
        shards,
        mesh=mesh,
        in_specs=(P("row", "col"), P("row"), P()),
        out_specs=(P("row", "col"), P("col", None)),
        check_vma=False,
    )
```

profile of v0, /device:TPU:0, one launch (start us, length us, event | category | flops | bytes accessed | tf_op | source)
XLA Modules:
  0.0 712.5 jit_solution(14026920130892729794)
XLA Ops:
  7.2 0.8 convert_element_type.30
  8.0 8.7 %broadcast_multiply_fusion.1 = f32[16384,128]{1,0:T(8,128)S(1)} fusion(f32[16384,128]{1,0:T(8,128)} %param.3, f32[16384]{0:T(1024)S(1)} %convert_element_type.30), kind=kLoop, calls=%fused_computation.10 | loop fusion | flops 2097152 | bytes 16842752 | tf_op jit(solution)/shard_map/mul | solution.py:31
  16.7 16.6 %convolution_bitcast_fusion = f32[64,256,128]{1,2,0:T(8,128)} fusion(f32[64,256,128]{2,1,0:T(8,128)S(1)} %bitcast.64), kind=kOutput, calls=%fused_computation.11 | convolution fusion | flops 6443433984 | bytes 16777216 | tf_op jit(solution)/shard_map/cj,ajp->acp/dot_general | solution.py:33
  33.3 8.7 %copy.9 = f32[64,256,128]{2,0,1:T(8,128)} copy(f32[64,256,128]{1,2,0:T(8,128)} %convolution_bitcast_fusion) | data formatting | bytes 16777216 | tf_op jit(solution)/shard_map/cj,ajp->acp/transpose | solution.py:33
  42.0 10.9 %broadcast_multiply_fusion = f32[64,256,128]{2,0,1:T(8,128)S(1)} fusion(f32[64,256,128]{2,0,1:T(8,128)} %copy.9), kind=kOutput, calls=%fused_computation.9 | convolution fusion | flops 1612771328 | bytes 16777216 | tf_op jit(solution)/shard_map/ba,acp->bcp/dot_general | solution.py:36
  52.9 8.1 %copy.10 = f32[64,256,128]{2,1,0:T(8,128)} copy(f32[64,256,128]{2,0,1:T(8,128)S(1)} %broadcast_multiply_fusion) | data formatting | bytes 16777216 | tf_op jit(solution)/shard_map/mul | solution.py:39
  61.0 7.4 %all-to-all-start = ((f32[8,2048,128]{2,1,0:T(8,128)}), f32[8,2048,128]{2,1,0:T(8,128)}, u32[]{:S(2)}, u32[]{:S(2)}) async-start(f32[8,2048,128]{2,1,0:T(8,128)} %bitcast.63), calls=%async_computation | async-start | bytes 16777216 | tf_op jit(solution)/shard_map/all_to_all | solution.py:47
  68.4 0.2 add_select_fusion.3
  68.6 0.1 fusion.79
  68.8 2.3 reduce-window.16
  71.1 0.3 slice_reduce_fusion
  71.4 0.2 reduce-window.19
  72.2 120.1 %scatter_custom_fusion.1 = s32[8192]{0:T(1024)S(1)} fusion(s32[32768]{0:T(1024)S(1)} %bitcast.67, s32[32768]{0:T(1024)S(1)} %bitcast.69, s32[]{:T(128)} %constant.142.clone.1), kind=kCustom, calls=%fused_computation.99 | custom fusion | bytes 32772
  192.3 61.7 %gather_fusion.3 = s32[8192]{0:T(1024)S(1)} fusion(s32[8,4096]{1,0:T(8,128)S(1)} %reshape.201, s32[8192]{0:T(1024)S(1)} %bitcast.60), kind=kCustom, calls=%fused_computation.3 | custom fusion | bytes 131072 | tf_op jit(solution)/shard_map/jit(take_along_axis)/gather | solution.py:73
  254.1 136.5 %scatter_custom_fusion = pred[8192]{0:T(1024)(128)(4,1)S(1)} fusion(s32[32768]{0:T(1024)S(1)} %bitcast.68, pred[32768]{0:T(1024)(128)(4,1)S(1)} %broadcast.265, pred[]{:T(512)} %constant.159.clone.1), kind=kCustom, calls=%fused_computation.108 | custom fusion | bytes 8193
  390.7 15.5 %fusion = f32[8,2048,128]{2,0,1:T(8,128)S(1)} fusion(f32[8,2048,128]{2,1,0:T(8,128)} %all-to-all-done), kind=kOutput, calls=%fused_computation.6 | convolution fusion | flops 201327552 | bytes 16777216 | tf_op jit(solution)/shard_map/ed,dkp->ekp/dot_general | solution.py:48
  406.3 4.7 copy.12
  411.0 31.1 %gather_fusion = f32[8192,128]{1,0:T(8,128)} fusion(f32[16384,128]{1,0:T(8,128)} %bitcast.62, s32[8192]{0:T(1024)S(1)} %broadcast_clamp_fusion), kind=kCustom, calls=%fused_computation | custom fusion | bytes 8421376 | tf_op jit(solution)/shard_map/jit(_take)/gather | solution.py:74
  442.1 7.7 %select_select_fusion = f32[8,1024,128]{2,1,0:T(8,128)} fusion(f32[8,1024,128]{2,1,0:T(8,128)} %bitcast.65, pred[8,1024]{1,0:T(8,128)(4,1)S(1)} %compare_and_fusion, pred[8,1024]{1,0:T(8,128)(4,1)S(1)} %reshape.209), kind=kLoop, calls=%fused_computation.8 | loop fusion | flops 2097152 | bytes 8404992 | tf_op jit(solution)/shard_map/jit(_where)/select_n | solution.py:77
  449.8 6.0 all-to-all-start.1
  455.9 2.3 reduce-window.14
  458.2 0.3 slice_reduce_fusion.1
  458.5 0.2 reduce-window.15
  459.0 24.5 %gather_fusion.2 = s32[4096]{0:T(1024)S(1)} fusion(s32[4096,8]{0,1:T(8,128)S(1)} %bitcast.59, s32[4096]{0:T(1024)S(1)} %bitcast.61), kind=kCustom, calls=%fused_computation.2 | custom fusion | bytes 65536 | tf_op jit(solution)/shard_map/jit(take_along_axis)/gather | solution.py:84
  483.6 64.9 %all-to-all-done.1 = f32[8,1024,128]{2,1,0:T(8,128)} async-done(((f32[8,1024,128]{2,1,0:T(8,128)}), f32[8,1024,128]{2,1,0:T(8,128)}, u32[]{:S(2)}, u32[]{:S(2)}) %all-to-all-start.1) | async-done | bytes 4194336 | tf_op jit(solution)/shard_map/all_to_all | solution.py:78
  548.5 13.0 %gather_fusion.1 = f32[4096,128]{1,0:T(8,128)S(1)} fusion(f32[8192,128]{1,0:T(8,128)} %bitcast.16, s32[4096]{0:T(1024)S(1)} %broadcast_clamp_fusion.1), kind=kCustom, calls=%fused_computation.1 | custom fusion | bytes 4210688 | tf_op jit(solution)/shard_map/jit(_take)/gather | solution.py:85
  561.4 3.1 broadcast_select_fusion
  564.6 0.3 all-reduce.2.cloned.1.call-start
  564.9 58.4 %all-gather.2.cloned.1.call-done = f32[4096,512]{1,0:T(8,128)} async-done(((f32[4096,128]{1,0:T(8,128)}), f32[4096,512]{1,0:T(8,128)}) %all-gather.2.cloned.1.call-update) | async-done | bytes 8388624 | tf_op jit(solution)/shard_map/all_gather | solution.py:88
  623.2 9.8 %fusion.81 = f32[128,512]{1,0:T(8,128)} fusion(f32[4096,128]{1,0:T(8,128)} %broadcast_select_fusion, f32[4096,512]{1,0:T(8,128)} %all-gather.2.cloned.1.call-done), kind=kOutput, calls=%fused_computation.148 | convolution fusion | flops 3221225472 | bytes 10747904 | tf_op jit(solution)/shard_map/dot_general | solution.py:89
  633.0 70.7 %all-reduce.2.cloned.1.call-done = f32[128,512]{1,0:T(8,128)} async-done(((f32[128,512]{1,0:T(8,128)}), f32[128,512]{1,0:T(8,128)}) %all-reduce.2.cloned.1.call-update) | async-done | bytes 262160 | tf_op jit(solution)/shard_map/psum | solution.py:92
  703.7 1.7 broadcast_multiply_fusion.2
  (42 shorter events, 1.2 us)
Async XLA Ops:
  61.0 7.4 %copy-start = (s32[32768]{0:T(1024)S(1)}, s32[32768]{0:T(1024)}, u32[]{:S(2)}) copy-start(s32[32768]{0:T(1024)} %param.5) | copy-start | bytes 393220
  61.0 10.8 %copy-start.2 = (s32[2]{0:T(128)S(1)}, s32[2]{0:T(128)}, u32[]{:S(2)}) copy-start(s32[2]{0:T(128)} %constant.171) | copy-start | bytes 28
  61.0 10.9 %copy-start.1 = (s32[2]{0:T(128)S(1)}, s32[2]{0:T(128)}, u32[]{:S(2)}) copy-start(s32[2]{0:T(128)} %constant.174) | copy-start | bytes 28
  61.0 329.7 %all-to-all-start = ((f32[8,2048,128]{2,1,0:T(8,128)}), f32[8,2048,128]{2,1,0:T(8,128)}, u32[]{:S(2)}, u32[]{:S(2)}) async-start(f32[8,2048,128]{2,1,0:T(8,128)} %bitcast.63), calls=%async_computation | async-start | bytes 16777216 | tf_op jit(solution)/shard_map/all_to_all | solution.py:47
  449.8 98.7 %all-to-all-start.1 = ((f32[8,1024,128]{2,1,0:T(8,128)}), f32[8,1024,128]{2,1,0:T(8,128)}, u32[]{:S(2)}, u32[]{:S(2)}) async-start(f32[8,1024,128]{2,1,0:T(8,128)} %select_select_fusion), calls=%async_computation.1 | async-start | bytes 8388608 | tf_op jit(solution)/shard_map/all_to_all | solution.py:78
  455.8 167.5 %all-gather.2.cloned.1.call-start = ((), (), s32[]{:S(2)}) async-start(), calls=%async_computation.2 | async-start | bytes 10485760 | tf_op jit(solution)/shard_map/all_gather | solution.py:88
  564.6 139.2 %all-reduce.2.cloned.1.call-start = ((), (), s32[]{:S(2)}) async-start(), calls=%async_computation.3 | async-start | bytes 524288 | tf_op jit(solution)/shard_map/psum | solution.py:92
Sparse Core Ops, SparseCore 0:
  564.7 58.4 all-gather.1
  633.2 70.5 all-reduce.1
where the time goes:
time: 714 us; the launch traced here: 712 us
  local copies, waits for them, and re-layouts  409 us (57%)
  waiting for transfers between devices  194 us (27%)
  matrix products  52.8 us (7%)
  other arithmetic  28.1 us (4%)
  between operations  14.6 us (2%)
  starting transfers between devices  13.7 us (2%)
    unnamed x16, local copies, waits for them, and re-layouts  257 us
    psum x1, waiting for transfers between devices, shards(): gram = lax.psum(partial_gram, 'row') / sample_total  70.7 us
    all_to_all x1, waiting for transfers between devices, shards(): lax.all_to_all(outgoing, 'row', split_axis=0, concat_axis=0, tiled=True)  64.9 us
    gather x2, local copies, waits for them, and re-layouts, shards(): pick_index = jnp.take_along_axis(flat_rows, table, axis=1)  61.7 us
    all_gather x1, waiting for transfers between devices, shards(): every_panel = lax.all_gather(sketch, 'col', axis=1, tiled=True)  58.4 us
    gather x1, local copies, waits for them, and re-layouts, shards(): jnp.take(combined, pick_index.reshape(-1), axis=0)  31.1 us
    gather x1, local copies, waits for them, and re-layouts, shards(): position = jnp.take_along_axis(ranks, my_owners[:, None], axis=1)[:, 0]  24.5 us
    dot_general x1, matrix products, shards(): jnp.einsum('cj,ajp->acp', sylvester(inner_len), shaped, precision=lax.Pre...  16.6 us
  transfers between devices with their start and end apart: 4, of which 3 were waited for; matrix products, arithmetic and copies ran while one was open for 49% of the time, Pallas kernels for 0%

commit v1 on v0

v1 whole, which is shorter than its diff:
```python
import functools
import math

import jax
import jax.numpy as jnp
import numpy as np
from jax import lax
from jax.experimental import pallas as pl
from jax.experimental.pallas import tpu as pltpu
from jax.sharding import PartitionSpec as P

INNER = 256
VMEM_LIMIT = 48 * 1024 * 1024


def sylvester(order):
    index = np.arange(order)
    bits = index[:, None] & index[None, :]
    parity = np.zeros_like(bits)
    while bits.any():
        parity ^= bits & 1
        bits >>= 1
    return (1 - 2 * parity).astype(np.float32)


def butterfly(values):
    values = list(values)
    step = 1
    while step < len(values):
        for start in range(0, len(values), 2 * step):
            for k in range(start, start + step):
                a, b = values[k], values[k + step]
                values[k], values[k + step] = a + b, a - b
        step *= 2
    return values


def transform_kernel(steps_in, outer, devices, scale, h_ref, signs_ref, x_ref, out_ref, held):
    t = pl.program_id(0)
    per = outer // steps_in
    rows_out = out_ref.shape[2]

    @pl.when(t < steps_in)
    def _():
        h = h_ref[...]
        for k in range(per):
            x = x_ref[k]
            high = x.astype(jnp.bfloat16)
            low = (x - high.astype(jnp.float32)).astype(jnp.bfloat16)
            both = jnp.concatenate([high, low], axis=1)
            signed = (h * signs_ref[k]).astype(jnp.bfloat16)
            y = jnp.dot(signed, both, preferred_element_type=jnp.float32)
            width = x.shape[1]
            held[t * per + k] = (y[:, :width] + y[:, width:]) * scale

    @pl.when(t >= steps_in)
    def _():
        rows = pl.ds(pl.multiple_of((t - steps_in) * rows_out, rows_out), rows_out)
        low = 8
        for g in range(outer // low):
            values = butterfly([held[g * low + j, rows, :] for j in range(low)])
            for j in range(low):
                held[g * low + j, rows, :] = values[j]
        for j in range(low):
            values = butterfly([held[k * low + j, rows, :] for k in range(outer // low)])
            for k in range(outer // low):
                a = k * low + j
                out_ref[a % devices, a // devices] = values[k]


def local_transform(panel, signs, devices, scale):
    rows, width = panel.shape
    outer = rows // INNER
    steps_in = outer // 4
    rows_out = 32
    steps_out = INNER // rows_out
    h = jnp.asarray(sylvester(INNER))
    return pl.pallas_call(
        functools.partial(transform_kernel, steps_in, outer, devices, scale),
        grid=(steps_in + steps_out,),
        in_specs=[
            pl.BlockSpec((INNER, INNER), lambda t: (0, 0)),
            pl.BlockSpec((4, 1, INNER), lambda t: (jnp.minimum(t, steps_in - 1), 0, 0)),
            pl.BlockSpec((4, INNER, width), lambda t: (jnp.minimum(t, steps_in - 1), 0, 0)),
        ],
        out_specs=pl.BlockSpec(
            (devices, outer // devices, rows_out, width),
            lambda t: (0, 0, jnp.maximum(t - steps_in, 0), 0),
        ),
        out_shape=jax.ShapeDtypeStruct((devices, outer // devices, INNER, width), jnp.float32),
        scratch_shapes=[pltpu.VMEM((outer, INNER, width), jnp.float32)],
        compiler_params=pltpu.CompilerParams(vmem_limit_bytes=VMEM_LIMIT),
        cost_estimate=pl.CostEstimate(
            flops=4 * rows * INNER * width, bytes_accessed=8 * rows * width, transcendentals=0
        ),
        name="local_transform",
    )(h, signs.astype(jnp.float32).reshape(outer, 1, INNER), panel.reshape(outer, INNER, width))


def copy_rows(index_ref, first, count, source, store):
    unroll = 16 if count % 16 == 0 else 8

    @pl.loop(0, count // unroll)
    def _(k):
        base = k * unroll
        for u in range(unroll):
            store(base + u, source[pl.ds(index_ref[first + base + u], 1), :])


def pick_kernel(steps_in, index_ref, x_ref, out_ref, held):
    t = pl.program_id(0)
    devices, block, _ = x_ref.shape
    chunk = 32 if devices <= 8 else 8
    total = steps_in * block

    @pl.when(t == 0)
    def _():
        held[pl.ds(0, 8), :] = jnp.zeros((8, held.shape[1]), jnp.float32)

    @pl.when(t < steps_in)
    def _():
        @pl.loop(0, block // chunk)
        def _(c):
            rows = pl.ds(pl.multiple_of(c * chunk, chunk), chunk)
            values = butterfly([x_ref[d, rows, :] for d in range(devices)])
            for e in range(devices):
                at = pl.multiple_of(8 + e * total + t * block + c * chunk, 8)
                held[pl.ds(at, chunk), :] = values[e]

    @pl.when(t >= steps_in)
    def _():
        count = out_ref.shape[1]

        def store(r, row):
            out_ref[0, pl.ds(r, 1), :] = row

        copy_rows(index_ref, (t - steps_in) * count, count, held, store)


def combine_and_pick(received, index, capacity):
    devices, block_len, width = received.shape
    block = min(block_len, 256)
    steps_in = block_len // block
    return pl.pallas_call(
        functools.partial(pick_kernel, steps_in),
        grid_spec=pltpu.PrefetchScalarGridSpec(
            num_scalar_prefetch=1,
            grid=(steps_in + devices,),
            in_specs=[
                pl.BlockSpec((devices, block, width), lambda t, i: (0, jnp.minimum(t, steps_in - 1), 0))
            ],
            out_specs=pl.BlockSpec(
                (1, capacity, width), lambda t, i: (jnp.maximum(t - steps_in, 0), 0, 0)
            ),
            scratch_shapes=[pltpu.VMEM((devices * block_len + 8, width), jnp.float32)],
        ),
        out_shape=jax.ShapeDtypeStruct((devices, capacity, width), jnp.float32),
        compiler_params=pltpu.CompilerParams(vmem_limit_bytes=VMEM_LIMIT),
        name="combine_and_pick",
    )(index.reshape(-1), received)


def place_kernel(index_ref, x_ref, out_ref):
    count = out_ref.shape[0]

    def store(r, row):
        out_ref[pl.ds(r, 1), :] = row

    copy_rows(index_ref, pl.program_id(0) * count, count, x_ref, store)


def place_rows(arrived, index):
    rows, width = arrived.shape
    slots = index.shape[0]
    count = min(slots, 512)
    return pl.pallas_call(
        place_kernel,
        grid_spec=pltpu.PrefetchScalarGridSpec(
            num_scalar_prefetch=1,
            grid=(slots // count,),
            in_specs=[pl.BlockSpec((rows, width), lambda t, i: (0, 0))],
            out_specs=pl.BlockSpec((count, width), lambda t, i: (t, 0)),
        ),
        out_shape=jax.ShapeDtypeStruct((slots, width), jnp.float32),
        compiler_params=pltpu.CompilerParams(vmem_limit_bytes=VMEM_LIMIT),
        name="place_rows",
    )(index, arrived)


def gram_of(picked, sample_total):
    count, width = picked.shape
    half = count // 2
    columns = lax.axis_size("col")
    devices = lax.axis_size("row")
    c = lax.axis_index("col")
    side = c // 2

    def swap(value, mask):
        return lax.ppermute(value, "col", [(i, i ^ mask) for i in range(columns)])

    def dot(a, b):
        return lax.dot_general(
            a, b, (((0,), (0,)), ((), ())), precision=lax.Precision.HIGH,
            preferred_element_type=jnp.float32,
        )

    mine = lax.dynamic_slice_in_dim(picked, side * half, half)
    theirs = lax.dynamic_slice_in_dim(picked, (1 - side) * half, half)
    across = swap(theirs, 2)
    beside = swap(picked, 1)
    diagonal = swap(across, 1)
    beside_half = lax.dynamic_slice_in_dim(beside, side * half, half)
    near = dot(picked, jnp.concatenate([picked, beside], axis=1))
    far = dot(mine, jnp.concatenate([across, diagonal], axis=1))
    for_other = dot(across, jnp.concatenate([mine, beside_half], axis=1))
    far = far + swap(for_other, 2)
    blocks = jnp.concatenate([near, far], axis=1).reshape(width, columns, width)
    blocks = blocks.transpose(1, 0, 2)
    ordered = [lax.dynamic_index_in_dim(blocks, c ^ j, 0, keepdims=False) for j in range(columns)]
    partial = jnp.concatenate(ordered, axis=1)
    if width % devices or (width // devices) % 8:
        return lax.psum(partial, "row") / sample_total
    pieces = partial.reshape(devices, width // devices, columns * width)
    pieces = lax.all_to_all(pieces, "row", split_axis=0, concat_axis=0, tiled=True)
    reduced = jnp.sum(pieces, axis=0) / sample_total
    spread = jnp.broadcast_to(reduced[None], pieces.shape)
    spread = lax.all_to_all(spread, "row", split_axis=0, concat_axis=0, tiled=True)
    return spread.reshape(width, columns * width)


def shards(panel, signs, samples):
    row_count, width = panel.shape
    devices = lax.axis_size("row")
    me = lax.axis_index("row")
    outer = row_count // INNER
    block_len = row_count // devices
    sample_total = samples.shape[0]
    slots = sample_total // devices
    scale = 1.0 / math.sqrt(float(row_count * devices))

    local_rows = local_transform(panel, signs, devices, scale)
    pieces = local_rows.reshape(devices, block_len, width)
    received = lax.all_to_all(pieces, "row", split_axis=0, concat_axis=0, tiled=True)

    table = samples.reshape(devices, slots)
    local = table % row_count
    owners = (local // INNER) % devices
    in_block = (local // (INNER * devices)) * INNER + local % INNER
    flat = (table // row_count) * block_len + in_block
    mine = owners == me
    rank = jnp.where(mine, jnp.cumsum(mine.astype(jnp.int32), axis=1) - 1, -1)
    ids = jnp.arange(devices, dtype=jnp.int32)
    onehot = owners[:, None, :] == ids[None, :, None]
    most = jnp.max(jnp.sum(onehot.astype(jnp.int32), axis=2))
    my_owners = lax.dynamic_index_in_dim(owners, me, 0, keepdims=False)
    my_onehot = my_owners[None, :] == ids[:, None]
    my_ranks = jnp.cumsum(my_onehot.astype(jnp.int32), axis=1) - 1
    position = jnp.sum(jnp.where(my_onehot, my_ranks, 0), axis=0)

    mean = slots / devices
    capacity = min(slots, -(-int(mean + 5.5 * math.sqrt(mean)) // 16) * 16)

    def pick_index(room):
        wanted = jnp.arange(room, dtype=jnp.int32)[None, :, None]
        return jnp.sum(jnp.where(rank[:, None, :] == wanted, flat[:, None, :] + 8, 0), axis=2)

    received, fast_index = lax.optimization_barrier((received, pick_index(capacity)))

    def exchange(picked, room):
        arrived = lax.all_to_all(picked, "row", split_axis=0, concat_axis=0, tiled=True)
        return arrived.reshape(devices * room, width), my_owners * room + position

    def fast(received):
        picked = combine_and_pick(received, fast_index, capacity)
        sketch = place_rows(*exchange(picked, capacity))
        return sketch, gram_of(picked.reshape(devices * capacity, width), sample_total)

    def general(received):
        combined = jnp.stack(butterfly([received[d] for d in range(devices)]))
        combined = combined.reshape(devices * block_len, width)
        index = pick_index(slots).reshape(-1)
        picked = jnp.take(combined, jnp.maximum(index - 8, 0), axis=0)
        picked = jnp.where((index >= 8)[:, None], picked, 0.0)
        arrived, places = exchange(picked.reshape(devices, slots, width), slots)
        sketch = jnp.take(arrived, places, axis=0)
        return sketch, gram_of(sketch, sample_total)

    return lax.cond(most <= capacity, fast, general, received)


def solution(mesh):
    return jax.shard_map(
        shards,
        mesh=mesh,
        in_specs=(P("row", "col"), P("row"), P()),
        out_specs=(P("row", "col"), P("col", None)),
        check_vma=False,
    )
```

time: 714 us -> 363 us (0.51)
  local copies, waits for them, and re-layouts: 409 us -> 7.75 us
  waiting for transfers between devices: 194 us -> 255 us
  matrix products: 52.8 us -> 9.39 us
  Pallas kernels: 0 us -> 37.8 us
  between operations: 14.6 us -> 1.41 us
  blocking collectives: 0 us -> 12.7 us
  other arithmetic: 28.1 us -> 19.1 us
    unnamed x16 -> x5, local copies, waits for them, and re-layouts: 257 us -> 2.62 us
    all_to_all x1, waiting for transfers between devices: 0.01 us -> 164 us  [shards(): lax.all_to_all(pieces, 'row', split_axis=0, concat_axis=0, tiled=True)]
    gather x5 -> x0, local copies, waits for them, and re-layouts: 130 us -> none  [the longest x2 61.7 us: shards(): pick_index = jnp.take_along_axis(flat_rows, table, axis=1)]
    psum x1 -> x0, waiting for transfers between devices: 70.7 us -> none  [shards(): gram = lax.psum(partial_gram, 'row') / sample_total]
    all_gather x1 -> x0, waiting for transfers between devices: 58.4 us -> none  [shards(): every_panel = lax.all_gather(sketch, 'col', axis=1, tiled=True)]
    dot_general x4 -> x3, matrix products: 52.8 us -> 9.39 us  [dot(): lax.dot_general(a, b, (((0,), (0,)), ((), ())), precision=lax.Precision.H...]
    pallas_call x0 -> x3, Pallas kernels: none -> 37.8 us  [the longest x1 17 us: local_transform(): pl.pallas_call(functools.partial(transform_kernel, steps_in, outer, devic...]
    ppermute x0 -> x4, waiting for transfers between devices: none -> 29.7 us  [swap(): return lax.ppermute(value, 'col', [(i, i ^ mask) for i in range(columns)])]
  transfers between devices with their start and end apart: 4 -> 7, of which waited for: 3 -> 4; matrix products, arithmetic and copies ran while one was open for 49% -> 8% of each run, Pallas kernels for 0% -> 2%
where the time goes in v1:
time: 363 us; the launch traced here: 362 us
  waiting for transfers between devices  255 us (70%)
  Pallas kernels  37.8 us (10%)
  other arithmetic  19.1 us (5%)
  starting transfers between devices  18.4 us (5%)
  blocking collectives  12.7 us (3%)
  matrix products  9.39 us (3%)
  local copies, waits for them, and re-layouts  7.75 us (2%)
    all_to_all x1, waiting for transfers between devices, shards(): lax.all_to_all(pieces, 'row', split_axis=0, concat_axis=0, tiled=True)  164 us
    all_to_all x1, waiting for transfers between devices, exchange(): lax.all_to_all(picked, 'row', split_axis=0, concat_axis=0, tiled=True)  59.3 us
    ppermute x4, waiting for transfers between devices, swap(): return lax.ppermute(value, 'col', [(i, i ^ mask) for i in range(columns)])  29.7 us
    pallas_call x1, Pallas kernels, local_transform(): pl.pallas_call(functools.partial(transform_kernel, steps_in, outer, devic...  17 us
    pallas_call x1, Pallas kernels, combine_and_pick(): pl.pallas_call(functools.partial(pick_kernel, steps_in), grid_spec=pltpu....  14.2 us
    all_to_all x1, blocking collectives, gram_of(): lax.all_to_all(pieces, 'row', split_axis=0, concat_axis=0, tiled=True)  12.7 us
    reduce_sum x1, other arithmetic, pick_index(): jnp.sum(jnp.where(rank[:, None, :] == wanted, flat[:, None, :] + 8, 0), a...  11.3 us
    dot_general x3, matrix products, dot(): lax.dot_general(a, b, (((0,), (0,)), ((), ())), precision=lax.Precision.H...  9.39 us
  transfers between devices with their start and end apart: 7, of which 4 were waited for; matrix products, arithmetic and copies ran while one was open for 8% of the time, Pallas kernels for 2%

profile of v1, /device:TPU:0, one launch (start us, length us, event | category | flops | bytes accessed | tf_op | source)
XLA Modules:
  0.0 361.8 jit_solution(11547873364166650960)
XLA Ops:
  0.6 0.8 convert_element_type.21
  1.5 0.9 copy-done
  2.4 17.0 %local_transform.1 = f32[8,8,256,128]{3,2,1,0:T(8,128)} custom-call(f32[256,256]{1,0:T(8,128)S(1)} %copy-done, f32[64,1,256]{2,1,0:T(1,128)S(1)} %bitcast.40, f32[64,256,128]{2,1,0:T(8,128)} %bitcast.43), custom_call_target="tpu_custom_call" | custom-call | flops 2147483648 | bytes 16777216 | tf_op jit(solution)/shard_map/local_transform/pallas_call | solution.py:78
  19.5 7.4 %all-to-all-start.6 = ((f32[8,2048,128]{2,1,0:T(8,128)}), f32[8,2048,128]{2,1,0:T(8,128)}, u32[]{:S(2)}, u32[]{:S(2)}) async-start(f32[8,2048,128]{2,1,0:T(8,128)} %bitcast.42), calls=%async_computation.6 | async-start | bytes 16777216 | tf_op jit(solution)/shard_map/all_to_all | solution.py:243
  27.1 2.3 reduce-window.16
  29.4 0.3 slice_reduce_fusion
  30.0 0.4 fusion.55
  30.4 2.3 reduce-window.14
  32.7 0.3 slice_reduce_fusion.1
  33.2 0.3 convert_reduce_fusion
  33.5 0.6 reduce_max.9
  35.0 11.3 %select_reduce_fusion.1 = s32[8,640]{1,0:T(8,128)S(1)} fusion(s32[8,4096]{1,0:T(8,128)S(1)} %get-tuple-element.214, s32[8,4096]{1,0:T(8,128)S(1)} %get-tuple-element.218), kind=kLoop, calls=%fused_computation.101 | loop fusion | flops 62909440 | bytes 282624 | tf_op jit(solution)/shard_map/reduce_sum | solution.py:265
  46.4 163.6 %all-to-all-done.6 = f32[8,2048,128]{2,1,0:T(8,128)} async-done(((f32[8,2048,128]{2,1,0:T(8,128)}), f32[8,2048,128]{2,1,0:T(8,128)}, u32[]{:S(2)}, u32[]{:S(2)}) %all-to-all-start.6) | async-done | bytes 8388640 | tf_op jit(solution)/shard_map/all_to_all | solution.py:243
  210.2 150.0 %conditional.1 = (f32[4096,128]{1,0:T(8,128)}, f32[128,512]{1,0:T(8,128)}) conditional(s32[]{:T(128)} %convert_element_type.18, (s32[4096]{0:T(1024)S(1)}, s32[4096]{0:T(1024)S(1)}, s32[]{:T(128)}, s32[8,4096]{1,0:T(8,128)S(1)}, s32[8,32,128]{2,1,0:T(8,128)S(1)}, /*index=5*/s32[8,32,128]{2,1,0:T(8,128)S(1)}, s32[8,4096]{1,0:T(8,128)S(1)}, ...), branch_computations={%region_8.11_spmd, %region_11.13_spmd} | conditional | flops 2034196480 | bytes 226697984 | solution.py:288
  210.4 14.2 %combine_and_pick.1 = f32[8,640,128]{2,1,0:T(8,128)} custom-call(s32[5120]{0:T(1024)S(1)} %reshape.305.index_ref, f32[8,2048,128]{2,1,0:T(8,128)} %get-tuple-element.118.x_ref), custom_call_target="tpu_custom_call" | custom-call | tf_op jit(solution)/shard_map/cond/branch_1_fun/combine_and_pick/pallas_call | solution.py:144
  224.7 1.9 constant_dynamic-slice_fusion.6
  226.6 1.6 collective-permute-start.5
  228.2 29.7 %collective-permute-done.5 = f32[2560,128]{1,0:T(8,128)S(1)} collective-permute-done((f32[2560,128]{1,0:T(8,128)S(1)}, f32[2560,128]{1,0:T(8,128)S(1)}, u32[]{:S(2)}, u32[]{:S(2)}) %collective-permute-start.5) | collective-permute-done | bytes 1310752 | tf_op jit(solution)/shard_map/cond/branch_1_fun/ppermute | solution.py:199
  257.8 1.4 constant_dynamic-slice_fusion.4
  259.2 1.3 fusion.8
  260.6 1.6 collective-permute-start.7
  262.2 5.5 %fusion = f32[128,256]{1,0:T(8,128)S(1)} fusion(f32[5120,128]{1,0:T(8,128)} %bitcast.10, f32[5120,128]{1,0:T(8,128)} %collective-permute-done.4), kind=kOutput, calls=%fused_computation.2 | convolution fusion | flops 1007943680 | bytes 5373952 | tf_op jit(solution)/shard_map/cond/branch_1_fun/dot_general | solution.py:202
  267.7 2.5 fusion.12
  270.4 0.2 constant_dynamic-slice_fusion.3
  270.7 12.7 %all_to_all.31 = f32[8,16,512]{2,1,0:T(8,128)S(1)} all-to-all(f32[8,16,512]{2,1,0:T(8,128)S(1)} %pad_maximum_fusion.1), channel_id=1, replica_groups=mesh['row'=8,'col'=4] {'row'}, dimensions={0} | all-to-all | bytes 524288 | tf_op jit(solution)/shard_map/cond/branch_1_fun/all_to_all | solution.py:224
  283.4 3.8 %all-to-all-start.3 = ((f32[8,640,128]{2,1,0:T(8,128)}), f32[8,640,128]{2,1,0:T(8,128)S(1)}, u32[]{:S(2)}, u32[]{:S(2)}) async-start(f32[8,640,128]{2,1,0:T(8,128)} %combine_and_pick.1), calls=%async_computation.3 | async-start | bytes 5242880 | tf_op jit(solution)/shard_map/cond/branch_1_fun/all_to_all | solution.py:270
  287.2 59.3 %all-to-all-done.3 = f32[8,640,128]{2,1,0:T(8,128)S(1)} async-done(((f32[8,640,128]{2,1,0:T(8,128)}), f32[8,640,128]{2,1,0:T(8,128)S(1)}, u32[]{:S(2)}, u32[]{:S(2)}) %all-to-all-start.3) | async-done | bytes 2621472 | tf_op jit(solution)/shard_map/cond/branch_1_fun/all_to_all | solution.py:270
  346.6 0.7 broadcast_in_dim.81
  347.3 4.0 %all-to-all-start.5 = ((f32[8,16,512]{2,1,0:T(8,128)}), f32[8,16,512]{2,1,0:T(8,128)}, u32[]{:S(2)}, u32[]{:S(2)}) async-start(f32[8,16,512]{2,1,0:T(8,128)} %broadcast_in_dim.81), calls=%async_computation.5 | async-start | bytes 524288 | tf_op jit(solution)/shard_map/cond/branch_1_fun/all_to_all | solution.py:227
  351.4 6.5 %place_rows.1 = f32[4096,128]{1,0:T(8,128)} custom-call(s32[4096]{0:T(1024)S(1)} %multiply_add_fusion.index_ref, f32[5120,128]{1,0:T(8,128)S(1)} %bitcast.39), custom_call_target="tpu_custom_call" | custom-call | tf_op jit(solution)/shard_map/cond/branch_1_fun/place_rows/pallas_call | solution.py:176
  357.8 2.3 all-to-all-done.5
  360.1 1.7 copy.35
  (33 shorter events, 1.3 us)
Async XLA Ops:
  1.5 0.9 copy-start
  19.5 7.4 %copy-start.1 = (s32[32768]{0:T(1024)S(1)}, s32[32768]{0:T(1024)}, u32[]{:S(2)}) copy-start(s32[32768]{0:T(1024)} %param.8) | copy-start | bytes 393220
  19.5 190.5 %all-to-all-start.6 = ((f32[8,2048,128]{2,1,0:T(8,128)}), f32[8,2048,128]{2,1,0:T(8,128)}, u32[]{:S(2)}, u32[]{:S(2)}) async-start(f32[8,2048,128]{2,1,0:T(8,128)} %bitcast.42), calls=%async_computation.6 | async-start | bytes 16777216 | tf_op jit(solution)/shard_map/all_to_all | solution.py:243
  210.4 14.3 %copy-start.2 = (s32[4096]{0:T(1024)}, s32[4096]{0:T(1024)S(1)}, u32[]{:S(2)}) copy-start(s32[4096]{0:T(1024)S(1)} %get-tuple-element.116) | copy-start | bytes 49156 | tf_op jit(solution)/shard_map/cond
  224.7 33.1 %collective-permute-start.4 = (f32[5120,128]{1,0:T(8,128)}, f32[5120,128]{1,0:T(8,128)}, u32[]{:S(2)}, u32[]{:S(2)}) collective-permute-start(f32[5120,128]{1,0:T(8,128)} %bitcast.10), channel_id=1, source_target_pairs={{0,1},{1,0},{2,3},{3,2},{4,5},{5,4},{6,7},{7,6},{8,9},{9,8},{10,11... | collective-permute-start | bytes 7864328 | tf_op jit(solution)/shard_map/cond/branch_1_fun/ppermute | solution.py:199
  226.6 31.3 %collective-permute-start.5 = (f32[2560,128]{1,0:T(8,128)S(1)}, f32[2560,128]{1,0:T(8,128)S(1)}, u32[]{:S(2)}, u32[]{:S(2)}) collective-permute-start(f32[2560,128]{1,0:T(8,128)S(1)} %get-tuple-element.199), channel_id=1, source_target_pairs={{0,2},{1,3},{2,0},{3,1},{4,6},{5,7},{6,4},{7,5},{8,10},{9,11},{10,... | collective-permute-start | bytes 3932168 | tf_op jit(solution)/shard_map/cond/branch_1_fun/ppermute | solution.py:199
  257.8 9.9 %collective-permute-start.6 = (f32[2560,128]{1,0:T(8,128)S(1)}, f32[2560,128]{1,0:T(8,128)}, u32[]{:S(2)}, u32[]{:S(2)}) collective-permute-start(f32[2560,128]{1,0:T(8,128)S(1)} %collective-permute-done.5), channel_id=1, source_target_pairs={{0,1},{1,0},{2,3},{3,2},{4,5},{5,4},{6,7},{7,6},{8,9},{9,8},{10,11... | collective-permute-start | bytes 3932168 | tf_op jit(solution)/shard_map/cond/branch_1_fun/ppermute | solution.py:199
  260.6 7.1 %collective-permute-start.7 = (f32[128,256]{1,0:T(8,128)S(1)}, f32[128,256]{1,0:T(8,128)S(1)}, u32[]{:S(2)}, u32[]{:S(2)}) collective-permute-start(f32[128,256]{1,0:T(8,128)S(1)} %fusion.8), channel_id=1, source_target_pairs={{0,2},{1,3},{2,0},{3,1},{4,6},{5,7},{6,4},{7,5},{8,10},{9,11},{10,... | collective-permute-start | bytes 393224 | tf_op jit(solution)/shard_map/cond/branch_1_fun/ppermute | solution.py:199
  283.4 67.9 %copy-start.3 = (s32[4096]{0:T(1024)S(1)}, s32[4096]{0:T(1024)}, u32[]{:S(2)}) copy-start(s32[4096]{0:T(1024)} %copy-done.2) | copy-start | bytes 49156 | tf_op jit(solution)/shard_map/cond
  283.4 63.1 %all-to-all-start.3 = ((f32[8,640,128]{2,1,0:T(8,128)}), f32[8,640,128]{2,1,0:T(8,128)S(1)}, u32[]{:S(2)}, u32[]{:S(2)}) async-start(f32[8,640,128]{2,1,0:T(8,128)} %combine_and_pick.1), calls=%async_computation.3 | async-start | bytes 5242880 | tf_op jit(solution)/shard_map/cond/branch_1_fun/all_to_all | solution.py:270
  347.3 12.8 %all-to-all-start.5 = ((f32[8,16,512]{2,1,0:T(8,128)}), f32[8,16,512]{2,1,0:T(8,128)}, u32[]{:S(2)}, u32[]{:S(2)}) async-start(f32[8,16,512]{2,1,0:T(8,128)} %broadcast_in_dim.81), calls=%async_computation.5 | async-start | bytes 524288 | tf_op jit(solution)/shard_map/cond/branch_1_fun/all_to_all | solution.py:227

commit v2 on v1

v2 whole, which is shorter than its diff:
```python
import functools
import math

import jax
import jax.numpy as jnp
import numpy as np
from jax import lax
from jax.experimental import pallas as pl
from jax.experimental.pallas import tpu as pltpu
from jax.sharding import PartitionSpec as P

INNER = 256
VMEM_LIMIT = 48 * 1024 * 1024


def sylvester(order):
    index = np.arange(order)
    bits = index[:, None] & index[None, :]
    parity = np.zeros_like(bits)
    while bits.any():
        parity ^= bits & 1
        bits >>= 1
    return (1 - 2 * parity).astype(np.float32)


def butterfly(values):
    values = list(values)
    step = 1
    while step < len(values):
        for start in range(0, len(values), 2 * step):
            for k in range(start, start + step):
                a, b = values[k], values[k + step]
                values[k], values[k + step] = a + b, a - b
        step *= 2
    return values


def transform_kernel(steps_in, outer, devices, scale, h_ref, signs_ref, x_ref, *refs):
    t = pl.program_id(0)
    *out_refs, held = refs
    per = outer // steps_in
    rows_out = out_refs[0].shape[2]
    members = devices // len(out_refs)

    @pl.when(t < steps_in)
    def _():
        h = h_ref[...]
        for k in range(per):
            x = x_ref[k]
            high = x.astype(jnp.bfloat16)
            low = (x - high.astype(jnp.float32)).astype(jnp.bfloat16)
            both = jnp.concatenate([high, low], axis=1)
            signed = (h * signs_ref[k]).astype(jnp.bfloat16)
            y = jnp.dot(signed, both, preferred_element_type=jnp.float32)
            width = x.shape[1]
            held[t * per + k] = (y[:, :width] + y[:, width:]) * scale

    @pl.when(t >= steps_in)
    def _():
        rows = pl.ds(pl.multiple_of((t - steps_in) * rows_out, rows_out), rows_out)
        low = 8
        for g in range(outer // low):
            values = butterfly([held[g * low + j, rows, :] for j in range(low)])
            for j in range(low):
                held[g * low + j, rows, :] = values[j]
        for j in range(low):
            values = butterfly([held[k * low + j, rows, :] for k in range(outer // low)])
            for k in range(outer // low):
                a = k * low + j
                owner = a % devices
                out_refs[owner // members][owner % members, a // devices] = values[k]


def local_transform(panel, signs, devices, chunks, scale):
    rows, width = panel.shape
    outer = rows // INNER
    steps_in = outer // 4
    rows_out = 32
    steps_out = INNER // rows_out
    h = jnp.asarray(sylvester(INNER))
    return pl.pallas_call(
        functools.partial(transform_kernel, steps_in, outer, devices, scale),
        grid=(steps_in + steps_out,),
        in_specs=[
            pl.BlockSpec((INNER, INNER), lambda t: (0, 0)),
            pl.BlockSpec((4, 1, INNER), lambda t: (jnp.minimum(t, steps_in - 1), 0, 0)),
            pl.BlockSpec((4, INNER, width), lambda t: (jnp.minimum(t, steps_in - 1), 0, 0)),
        ],
        out_specs=[
            pl.BlockSpec(
                (devices // chunks, outer // devices, rows_out, width),
                lambda t: (0, 0, jnp.maximum(t - steps_in, 0), 0),
            )
        ]
        * chunks,
        out_shape=[
            jax.ShapeDtypeStruct((devices // chunks, outer // devices, INNER, width), jnp.float32)
        ]
        * chunks,
        scratch_shapes=[pltpu.VMEM((outer, INNER, width), jnp.float32)],
        compiler_params=pltpu.CompilerParams(vmem_limit_bytes=VMEM_LIMIT),
        cost_estimate=pl.CostEstimate(
            flops=4 * rows * INNER * width, bytes_accessed=8 * rows * width, transcendentals=0
        ),
        name="local_transform",
    )(h, signs.astype(jnp.float32).reshape(outer, 1, INNER), panel.reshape(outer, INNER, width))


def copy_rows(index_ref, first, count, source, store):
    unroll = 16 if count % 16 == 0 else 8

    @pl.loop(0, count // unroll)
    def _(k):
        base = k * unroll
        for u in range(unroll):
            store(base + u, source[pl.ds(index_ref[first + base + u], 1), :])


def pick_kernel(steps_in, index_ref, sign_ref, x_ref, out_ref, held):
    t = pl.program_id(0)
    members, block, _ = x_ref.shape
    chunk = 32 if members <= 8 else 8
    total = steps_in * block

    @pl.when(t == 0)
    def _():
        held[pl.ds(0, 8), :] = jnp.zeros((8, held.shape[1]), jnp.float32)

    @pl.when(t < steps_in)
    def _():
        sign = sign_ref[0].astype(jnp.float32)

        @pl.loop(0, block // chunk)
        def _(c):
            rows = pl.ds(pl.multiple_of(c * chunk, chunk), chunk)
            values = butterfly([x_ref[d, rows, :] for d in range(members)])
            for e in range(2 * members):
                at = pl.multiple_of(8 + e * total + t * block + c * chunk, 8)
                value = values[e] if e < members else values[e - members] * sign
                held[pl.ds(at, chunk), :] = value

    @pl.when(t >= steps_in)
    def _():
        count = out_ref.shape[1]

        def store(r, row):
            out_ref[0, pl.ds(r, 1), :] = row

        copy_rows(index_ref, (t - steps_in) * count, count, held, store)


def combine_and_pick(received, index, sign, capacity):
    members, block_len, width = received.shape
    devices = 2 * members
    block = min(block_len, 256)
    steps_in = block_len // block
    return pl.pallas_call(
        functools.partial(pick_kernel, steps_in),
        grid_spec=pltpu.PrefetchScalarGridSpec(
            num_scalar_prefetch=2,
            grid=(steps_in + devices,),
            in_specs=[
                pl.BlockSpec(
                    (members, block, width), lambda t, i, g: (0, jnp.minimum(t, steps_in - 1), 0)
                )
            ],
            out_specs=pl.BlockSpec(
                (1, capacity, width), lambda t, i, g: (jnp.maximum(t - steps_in, 0), 0, 0)
            ),
            scratch_shapes=[pltpu.VMEM((devices * block_len + 8, width), jnp.float32)],
        ),
        out_shape=jax.ShapeDtypeStruct((devices, capacity, width), jnp.float32),
        compiler_params=pltpu.CompilerParams(vmem_limit_bytes=VMEM_LIMIT),
        cost_estimate=pl.CostEstimate(
            flops=8 * devices * block_len * width,
            bytes_accessed=16 * devices * block_len * width,
            transcendentals=0,
        ),
        name="combine_and_pick",
    )(index.reshape(-1), sign.reshape(1), received)


def place_kernel(index_ref, *refs):
    *x_refs, out_ref, held = refs
    count = out_ref.shape[0]
    rows = x_refs[0].shape[0]

    @pl.when(pl.program_id(0) == 0)
    def _():
        for k, x_ref in enumerate(x_refs):
            @pl.loop(0, rows // 16)
            def _(c):
                at = pl.multiple_of(c * 16, 16)
                held[pl.ds(k * rows + at, 16), :] = x_ref[pl.ds(at, 16), :]

    def store(r, row):
        out_ref[pl.ds(r, 1), :] = row

    copy_rows(index_ref, pl.program_id(0) * count, count, held, store)


def place_rows(arrived, index):
    rows, width = arrived[0].shape
    slots = index.shape[0]
    count = min(slots, 512)
    return pl.pallas_call(
        place_kernel,
        grid_spec=pltpu.PrefetchScalarGridSpec(
            num_scalar_prefetch=1,
            grid=(slots // count,),
            in_specs=[pl.BlockSpec((rows, width), lambda t, i: (0, 0))] * len(arrived),
            out_specs=pl.BlockSpec((count, width), lambda t, i: (t, 0)),
            scratch_shapes=[pltpu.VMEM((rows * len(arrived), width), jnp.float32)],
        ),
        out_shape=jax.ShapeDtypeStruct((slots, width), jnp.float32),
        compiler_params=pltpu.CompilerParams(vmem_limit_bytes=VMEM_LIMIT),
        name="place_rows",
    )(index, *arrived)


def swap_columns(value, mask):
    columns = lax.axis_size("col")
    return lax.ppermute(value, "col", [(i, i ^ mask) for i in range(columns)])


def gram_terms(picked):
    half = picked.shape[0] // 2
    side = lax.axis_index("col") // 2

    def dot(a, b):
        return lax.dot_general(
            a, b, (((0,), (0,)), ((), ())), precision=lax.Precision.HIGH,
            preferred_element_type=jnp.float32,
        )

    mine = lax.dynamic_slice_in_dim(picked, side * half, half)
    theirs = lax.dynamic_slice_in_dim(picked, (1 - side) * half, half)
    across = swap_columns(theirs, 2)
    beside = swap_columns(picked, 1)
    diagonal = swap_columns(across, 1)
    beside_half = lax.dynamic_slice_in_dim(beside, side * half, half)
    near = dot(picked, jnp.concatenate([picked, beside], axis=1))
    far = dot(mine, jnp.concatenate([across, diagonal], axis=1))
    for_other = dot(across, jnp.concatenate([mine, beside_half], axis=1))
    return near, far, for_other


def gram_from(terms, sample_total, after):
    near, far, for_other = terms
    columns = lax.axis_size("col")
    c = lax.axis_index("col")
    width = near.shape[0]
    far = far + swap_columns(for_other, 2)
    blocks = jnp.concatenate([near, far], axis=1).reshape(width, columns, width)
    blocks = blocks.transpose(1, 0, 2)
    ordered = [lax.dynamic_index_in_dim(blocks, c ^ j, 0, keepdims=False) for j in range(columns)]
    partial = jnp.concatenate(ordered, axis=1)
    devices = lax.axis_size("row")
    if after is None or devices & (devices - 1) or width % (8 * devices):
        return sum_over_rows(partial) / sample_total
    return reduce_rows(partial, after, 1.0 / sample_total)


def reduce_kernel(scale, x_ref, *refs):
    out_ref, came, total, gathered, send_in, recv_in, send_out, recv_out = refs[-8:]
    devices = x_ref.shape[0]
    me = lax.axis_index("row")
    mesh_id = pl.DeviceIdType.MESH
    barrier = pltpu.get_barrier_semaphore()
    for m in range(1, devices):
        pl.semaphore_signal(barrier, inc=1, device_id={"row": me ^ m}, device_id_type=mesh_id)
    pl.semaphore_wait(barrier, devices - 1)
    copies = []
    for m in range(1, devices):
        copy = pltpu.make_async_remote_copy(
            src_ref=x_ref.at[me ^ m], dst_ref=came.at[m], send_sem=send_in.at[m],
            recv_sem=recv_in.at[m], device_id={"row": me ^ m}, device_id_type=mesh_id,
        )
        copy.start()
        copies.append(copy)
    value = x_ref[me]
    for m in range(1, devices):
        copies[m - 1].wait_recv()
        value = value + came[m]
    value = value * scale
    total[...] = value
    copies_out = []
    for m in range(1, devices):
        copy = pltpu.make_async_remote_copy(
            src_ref=total, dst_ref=gathered.at[m], send_sem=send_out.at[m],
            recv_sem=recv_out.at[m], device_id={"row": me ^ m}, device_id_type=mesh_id,
        )
        copy.start()
        copies_out.append(copy)
    out_ref[me] = value
    for m in range(1, devices):
        copies_out[m - 1].wait_recv()
        out_ref[me ^ m] = gathered[m]
    for copy in copies + copies_out:
        copy.wait_send()


def reduce_rows(partial, after, scale):
    devices = lax.axis_size("row")
    rows, columns = partial.shape
    part = (devices, rows // devices, columns)
    out = pl.pallas_call(
        functools.partial(reduce_kernel, scale),
        in_specs=[pl.BlockSpec(memory_space=pltpu.VMEM)]
        + [pl.BlockSpec(memory_space=pl.ANY)] * len(after),
        out_specs=pl.BlockSpec(memory_space=pltpu.VMEM),
        out_shape=jax.ShapeDtypeStruct(part, jnp.float32),
        scratch_shapes=[
            pltpu.VMEM(part, jnp.float32),
            pltpu.VMEM(part[1:], jnp.float32),
            pltpu.VMEM(part, jnp.float32),
        ]
        + [pltpu.SemaphoreType.DMA((devices,))] * 4,
        compiler_params=pltpu.CompilerParams(
            collective_id=0, has_side_effects=True, vmem_limit_bytes=VMEM_LIMIT
        ),
        name="reduce_rows",
    )(partial.reshape(part), *after)
    return out.reshape(rows, columns)


def sum_over_rows(value):
    devices = lax.axis_size("row")
    me = lax.axis_index("row")
    if devices & (devices - 1) or value.shape[0] % devices:
        return lax.psum(value, "row")

    def swap(part, mask):
        return lax.ppermute(part, "row", [(i, i ^ mask) for i in range(devices)])

    masks = [1 << k for k in range(devices.bit_length() - 1)]
    for mask in masks:
        half = value.shape[0] // 2
        upper = (me & mask) != 0
        low, high = value[:half], value[half:]
        value = jnp.where(upper, high, low) + swap(jnp.where(upper, low, high), mask)
    for mask in reversed(masks):
        upper = (me & mask) != 0
        other = swap(value, mask)
        low, high = jnp.where(upper, other, value), jnp.where(upper, value, other)
        value = jnp.concatenate([low, high], axis=0)
    return value


def shards(panel, signs, samples):
    row_count, width = panel.shape
    devices = lax.axis_size("row")
    members = devices // 2
    me = lax.axis_index("row")
    half, member = me // members, me % members
    outer = row_count // INNER
    block_len = row_count // devices
    sample_total = samples.shape[0]
    slots = sample_total // devices
    scale = 1.0 / math.sqrt(float(row_count * devices))
    groups = [list(range(members)), list(range(members, devices))]

    local_rows = local_transform(panel, signs, devices, 2, scale)
    pieces = [chunk.reshape(members, block_len, width) for chunk in local_rows]

    table = samples.reshape(devices, slots)
    local = table % row_count
    owners = (local // INNER) % devices
    in_block = (local // (INNER * devices)) * INNER + local % INNER
    flat = (table // row_count) * block_len + in_block
    ids = jnp.arange(devices, dtype=jnp.int32)
    onehot = owners[:, None, :] == ids[None, :, None]
    most = jnp.max(jnp.sum(onehot.astype(jnp.int32), axis=2))
    my_owners = lax.dynamic_index_in_dim(owners, me, 0, keepdims=False)
    my_onehot = my_owners[None, :] == ids[:, None]
    my_ranks = jnp.cumsum(my_onehot.astype(jnp.int32), axis=1) - 1
    position = jnp.sum(jnp.where(my_onehot, my_ranks, 0), axis=0)

    mean = slots / devices
    capacity = min(slots, -(-int(mean + 5.5 * math.sqrt(mean)) // 16) * 16)

    def pick_index(owner, room):
        mine = owners == owner
        rank = jnp.where(mine, jnp.cumsum(mine.astype(jnp.int32), axis=1) - 1, -1)
        wanted = jnp.arange(room, dtype=jnp.int32)[None, :, None]
        return jnp.sum(jnp.where(rank[:, None, :] == wanted, flat[:, None, :] + 8, 0), axis=2)

    def within(value):
        return lax.all_to_all(
            value, "row", split_axis=0, concat_axis=0, tiled=True, axis_index_groups=groups
        )

    def exchange_blocks(blocks):
        came = []
        for m in range(members):
            block = lax.dynamic_index_in_dim(blocks, member ^ m, 0, keepdims=False)
            if m:
                block = lax.ppermute(block, "row", [(i, i ^ m) for i in range(devices)])
            came.append(block)
        return came

    indices = [pick_index(k * members + member, capacity) for k in range(len(pieces))]
    first, *indices = lax.optimization_barrier((within(pieces[0]), *indices))

    def fast(*pieces):
        sign = 1 - 2 * half
        arrived, terms = [], None
        for k, piece in enumerate(pieces):
            received = within(piece) if k else first
            index = indices[k]
            picked = combine_and_pick(received, index, sign, capacity)
            kept = lax.dynamic_slice_in_dim(picked, half * members, members)
            sent = lax.dynamic_slice_in_dim(picked, (1 - half) * members, members)
            partner = [(i, (i + members) % devices) for i in range(devices)]
            whole = kept + lax.ppermute(sent, "row", partner)
            new = gram_terms(whole.reshape(members * capacity, width))
            terms = new if terms is None else [a + b for a, b in zip(terms, new)]
            arrived += exchange_blocks(whole)
        source = (my_owners // members) * members + ((my_owners % members) ^ member)
        sketch = place_rows(arrived, source * capacity + position)
        return sketch, gram_from(terms, sample_total, arrived)

    def general(*pieces):
        received = lax.all_to_all(
            jnp.concatenate(pieces), "row", split_axis=0, concat_axis=0, tiled=True
        )
        combined = jnp.stack(butterfly([received[d] for d in range(devices)]))
        combined = combined.reshape(devices * block_len, width)
        index = pick_index(me, slots).reshape(-1)
        picked = jnp.take(combined, jnp.maximum(index - 8, 0), axis=0)
        picked = jnp.where((index >= 8)[:, None], picked, 0.0)
        arrived = lax.all_to_all(
            picked.reshape(devices, slots, width), "row", split_axis=0, concat_axis=0, tiled=True
        )
        places = my_owners * slots + position
        sketch = jnp.take(arrived.reshape(devices * slots, width), places, axis=0)
        return sketch, gram_from(gram_terms(sketch), sample_total, None)

    return lax.cond(most <= capacity, fast, general, *pieces)


def solution(mesh):
    return jax.shard_map(
        shards,
        mesh=mesh,
        in_specs=(P("row", "col"), P("row"), P()),
        out_specs=(P("row", "col"), P("col", None)),
        check_vma=False,
    )
```

time: 363 us -> 304 us (0.84)
  waiting for transfers between devices: 255 us -> 150 us
  Pallas kernels: 37.8 us -> 65.2 us
  other arithmetic: 19.1 us -> 37.4 us
  blocking collectives: 12.7 us -> 0 us
  local copies, waits for them, and re-layouts: 7.75 us -> 15.5 us
  starting transfers between devices: 18.4 us -> 23.5 us
    all_to_all x3 -> x2, waiting for transfers between devices: 225 us -> 73.3 us  [within(): lax.all_to_all(value, 'row', split_axis=0, concat_axis=0, tiled=True, axi...]
    ppermute x4 -> x15, waiting for transfers between devices: 29.7 us -> 76.6 us  [the longest x2 53.9 us: fast(): whole = kept + lax.ppermute(sent, 'row', partner)]
    pallas_call x0 -> x1, Pallas kernels: none -> 16.5 us  [reduce_rows(): pl.pallas_call(functools.partial(reduce_kernel, scale), in_specs=[pl.Bloc...]
    all_to_all x1 -> x0, blocking collectives: 12.7 us -> none  [gram_of(): lax.all_to_all(pieces, 'row', split_axis=0, concat_axis=0, tiled=True)]
    reduce_sum x1, other arithmetic: 11.3 us -> 22.6 us  [pick_index(): jnp.sum(jnp.where(rank[:, None, :] == wanted, flat[:, None, :] + 8, 0), a...]
    ppermute x4 -> x15, starting transfers between devices: 3.19 us -> 13.3 us  [the longest x6 7.81 us: exchange_blocks(): block = lax.ppermute(block, 'row', [(i, i ^ m) for i in range(devices)])]
    pallas_call x1 -> x2, Pallas kernels: 14.2 us -> 23 us  [combine_and_pick(): pl.pallas_call(functools.partial(pick_kernel, steps_in), grid_spec=pltpu....]
    all_to_all x3 -> x2, starting transfers between devices: 15.2 us -> 10.2 us  [within(): lax.all_to_all(value, 'row', split_axis=0, concat_axis=0, tiled=True, axi...]
  transfers between devices with their start and end apart: 7 -> 17, of which waited for: 4 -> 8; matrix products, arithmetic and copies ran while one was open for 8% -> 18% of each run, Pallas kernels for 2% -> 10%
where the time goes in v2:
time: 304 us; the launch traced here: 303 us
  waiting for transfers between devices  150 us (49%)
  Pallas kernels  65.2 us (21%)
  other arithmetic  37.4 us (12%)
  starting transfers between devices  23.5 us (8%)
  local copies, waits for them, and re-layouts  15.5 us (5%)
  matrix products  9.67 us (3%)
    all_to_all x2, waiting for transfers between devices, within(): lax.all_to_all(value, 'row', split_axis=0, concat_axis=0, tiled=True, axi...  73.3 us
    ppermute x2, waiting for transfers between devices, fast(): whole = kept + lax.ppermute(sent, 'row', partner)  53.9 us
    pallas_call x2, Pallas kernels, combine_and_pick(): pl.pallas_call(functools.partial(pick_kernel, steps_in), grid_spec=pltpu....  23 us
    ppermute x6, waiting for transfers between devices, exchange_blocks(): block = lax.ppermute(block, 'row', [(i, i ^ m) for i in range(devices)])  22.6 us
    reduce_sum x1, other arithmetic, pick_index(): jnp.sum(jnp.where(rank[:, None, :] == wanted, flat[:, None, :] + 8, 0), a...  22.6 us
    pallas_call x1, Pallas kernels, local_transform(): pl.pallas_call(functools.partial(transform_kernel, steps_in, outer, devic...  17.2 us
    pallas_call x1, Pallas kernels, reduce_rows(): pl.pallas_call(functools.partial(reduce_kernel, scale), in_specs=[pl.Bloc...  16.5 us
    all_to_all x2, starting transfers between devices, within(): lax.all_to_all(value, 'row', split_axis=0, concat_axis=0, tiled=True, axi...  10.2 us
  transfers between devices with their start and end apart: 17, of which 8 were waited for; matrix products, arithmetic and copies ran while one was open for 18% of the time, Pallas kernels for 10%

profile of v2, /device:TPU:0, one launch (start us, length us, event | category | flops | bytes accessed | tf_op | source)
XLA Modules:
  0.0 302.9 jit_solution(5436456259183634147)
XLA Ops:
  2.4 17.2 %local_transform.1 = (f32[4,8,256,128]{3,2,1,0:T(8,128)}, f32[4,8,256,128]{3,2,1,0:T(8,128)}) custom-call(f32[256,256]{1,0:T(8,128)S(1)} %copy-done.1, f32[64,1,256]{2,1,0:T(1,128)S(1)} %bitcast.77, f32[64,256,128]{2,1,0:T(8,128)} %bitcast.86), custom_call_target="tpu_custom_call" | custom-call | flops 2147483648 | bytes 16777216 | tf_op jit(solution)/shard_map/local_transform/pallas_call | solution.py:81
  19.6 5.4 %all-to-all-start.3 = ((f32[4,2048,128]{2,1,0:T(8,128)}), f32[4,2048,128]{2,1,0:T(8,128)}, u32[]{:S(2)}, u32[]{:S(2)}) async-start(f32[4,2048,128]{2,1,0:T(8,128)} %bitcast.82), calls=%async_computation.3 | async-start | bytes 8388608 | tf_op jit(solution)/shard_map/all_to_all | solution.py:389
  25.2 2.3 reduce-window.30
  28.2 2.3 reduce-window.34
  31.7 2.3 reduce-window.26
  36.3 22.6 %select_reduce_fusion.1 = (s32[8,640]{1,0:T(8,128)S(1)}, s32[8,640]{1,0:T(8,128)S(1)}) fusion(s32[8,4096]{1,0:T(8,128)S(1)} %bitcast_select_fusion.1, s32[8,4096]{1,0:T(8,128)S(1)} %get-tuple-element.207, s32[8,4096]{1,0:T(8,128)S(1)} %get-tuple-element.211), kind=kLoop, calls=%fused_computation.164 | loop fusion | flops 125818880 | bytes 434176 | tf_op jit(solution)/shard_map/reduce_sum | solution.py:386
  58.8 14.7 %all-to-all-done.3 = f32[4,2048,128]{2,1,0:T(8,128)} async-done(((f32[4,2048,128]{2,1,0:T(8,128)}), f32[4,2048,128]{2,1,0:T(8,128)}, u32[]{:S(2)}, u32[]{:S(2)}) %all-to-all-start.3) | async-done | bytes 4194336 | tf_op jit(solution)/shard_map/all_to_all | solution.py:389
  73.6 228.7 %conditional.1 = (f32[4096,128]{1,0:T(8,128)}, f32[128,512]{1,0:T(8,128)S(1)}) conditional(s32[]{:T(128)} %convert_element_type.23, (s32[4096]{0:T(1024)S(1)}, s32[4096]{0:T(1024)S(1)}, s32[]{:T(128)}, s32[8,4096]{1,0:T(8,128)S(1)}, s32[8,4096]{1,0:T(8,128)S(1)}, /*index=5*/s32[8,4096]{1,0:T(8,128)S(1)}, s32[8,4096]{1,0:T(8,128)S(1)}, ...), branch_computations={%region_11.15_spmd, %region_15.16_spmd} | conditional | flops 2050588672 | bytes 273070144 | solution.py:439
  74.2 4.8 %all-to-all-start.2 = ((f32[4,2048,128]{2,1,0:T(8,128)}), f32[4,2048,128]{2,1,0:T(8,128)}, u32[]{:S(2)}, u32[]{:S(2)}) async-start(f32[4,2048,128]{2,1,0:T(8,128)} %get-tuple-element.145), calls=%async_computation.2 | async-start | bytes 8388608 | tf_op jit(solution)/shard_map/cond/branch_1_fun/all_to_all | solution.py:389
  79.1 11.5 %combine_and_pick.2 = f32[8,640,128]{2,1,0:T(8,128)S(1)} custom-call(s32[5120]{0:T(1024)S(1)} %reshape.347.index_ref, s32[1]{0:T(128)} %bitcast.8.sign_ref, f32[4,2048,128]{2,1,0:T(8,128)} %get-tuple-element.143.x_ref), custom_call_target="tpu_custom_call" | custom-call | flops 16777216 | bytes 33554432 | tf_op jit(solution)/shard_map/cond/branch_1_fun/combine_and_pick/pallas_call | solution.py:157
  93.3 2.8 collective-permute-start.10
  96.0 58.6 %all-to-all-done.2.x_ref = f32[4,2048,128]{2,1,0:T(8,128)} async-done(((f32[4,2048,128]{2,1,0:T(8,128)}), f32[4,2048,128]{2,1,0:T(8,128)}, u32[]{:S(2)}, u32[]{:S(2)}) %all-to-all-start.2) | async-done | bytes 4194336 | tf_op jit(solution)/shard_map/cond/branch_1_fun/all_to_all | solution.py:389
  154.6 11.5 %combine_and_pick.3 = f32[8,640,128]{2,1,0:T(8,128)S(1)} custom-call(s32[5120]{0:T(1024)S(1)} %reshape.349.index_ref, s32[1]{0:T(128)} %bitcast.8.sign_ref, f32[4,2048,128]{2,1,0:T(8,128)} %all-to-all-done.2.x_ref), custom_call_target="tpu_custom_call" | custom-call | flops 16777216 | bytes 33554432 | tf_op jit(solution)/shard_map/cond/branch_1_fun/combine_and_pick/pallas_call | solution.py:157
  167.3 1.8 dynamic-slice_add_fusion.1
  169.3 1.8 collective-permute-start.11
  171.1 53.9 %collective-permute-done.14 = f32[4,640,128]{2,1,0:T(8,128)} collective-permute-done((f32[4,640,128]{2,1,0:T(8,128)}, f32[4,640,128]{2,1,0:T(8,128)}, u32[]{:S(2)}, u32[]{:S(2)}) %collective-permute-start.14) | collective-permute-done | bytes 1310752 | tf_op jit(solution)/shard_map/cond/branch_1_fun/ppermute | solution.py:415
  225.0 2.5 dynamic-slice_add_fusion
  227.7 1.9 collective-permute-start.20
  229.6 2.5 collective-permute-start.13
  232.1 2.4 constant_dynamic-slice_fusion.7
  234.5 5.5 %collective-permute-done.12.refs_2_ = f32[640,128]{1,0:T(8,128)S(1)} collective-permute-done((f32[640,128]{1,0:T(8,128)S(1)}, f32[640,128]{1,0:T(8,128)S(1)}, u32[]{:S(2)}, u32[]{:S(2)}) %collective-permute-start.12) | collective-permute-done | bytes 327712 | tf_op jit(solution)/shard_map/cond/branch_1_fun/ppermute | solution.py:398
  240.3 2.3 dynamic-slice_bitcast_fusion
  242.6 4.4 %collective-permute-done.13.refs_3_ = f32[640,128]{1,0:T(8,128)S(1)} collective-permute-done((f32[640,128]{1,0:T(8,128)S(1)}, f32[640,128]{1,0:T(8,128)S(1)}, u32[]{:S(2)}, u32[]{:S(2)}) %collective-permute-start.13) | collective-permute-done | bytes 327712 | tf_op jit(solution)/shard_map/cond/branch_1_fun/ppermute | solution.py:398
  249.0 2.3 collective-permute-start.17
  252.5 3.7 %collective-permute-done.15.refs_5_ = f32[640,128]{1,0:T(8,128)S(1)} collective-permute-done((f32[640,128]{1,0:T(8,128)}, f32[640,128]{1,0:T(8,128)S(1)}, u32[]{:S(2)}, u32[]{:S(2)}) %collective-permute-start.15) | collective-permute-done | bytes 327712 | tf_op jit(solution)/shard_map/cond/branch_1_fun/ppermute | solution.py:398
  256.2 3.4 %collective-permute-done.16.refs_6_ = f32[640,128]{1,0:T(8,128)S(1)} collective-permute-done((f32[640,128]{1,0:T(8,128)}, f32[640,128]{1,0:T(8,128)S(1)}, u32[]{:S(2)}, u32[]{:S(2)}) %collective-permute-start.16) | collective-permute-done | bytes 327712 | tf_op jit(solution)/shard_map/cond/branch_1_fun/ppermute | solution.py:398
  259.6 5.6 %collective-permute-done.17.refs_7_ = f32[640,128]{1,0:T(8,128)S(1)} collective-permute-done((f32[640,128]{1,0:T(8,128)}, f32[640,128]{1,0:T(8,128)S(1)}, u32[]{:S(2)}, u32[]{:S(2)}) %collective-permute-start.17) | collective-permute-done | bytes 327712 | tf_op jit(solution)/shard_map/cond/branch_1_fun/ppermute | solution.py:398
  265.2 8.6 %place_rows.1 = f32[4096,128]{1,0:T(8,128)} custom-call(s32[4096]{0:T(1024)S(1)} %fusion.39.index_ref, f32[640,128]{1,0:T(8,128)S(1)} %get-tuple-element.188.refs_0_, f32[640,128]{1,0:T(8,128)S(1)} %collective-permute-done.11.refs_1_, f32[640,128]{1,0:T(8,128)S(1)} %collective-permute-done.12.refs_2_, f32[640,128]{1,0:T(8,128)S(1)} %collective-permute-done.13.refs_3_, ...), custom_call_target="tpu_custom_call" | custom-call | tf_op jit(solution)/shard_map/cond/branch_1_fun/place_rows/pallas_call | solution.py:206
  275.0 1.8 fusion.20
  278.1 3.3 %fusion.4 = f32[128,256]{1,0:T(8,128)S(1)} fusion(f32[2560,128]{1,0:T(8,128)} %bitcast.18, f32[2560,128]{1,0:T(8,128)} %collective-permute-done.19), kind=kOutput, calls=%fused_computation.6 | convolution fusion | flops 503971840 | bytes 2752512 | tf_op jit(solution)/shard_map/cond/branch_1_fun/dot_general | solution.py:231
  282.8 1.8 fusion.12
  285.8 16.5 %reduce_rows.1 = f32[8,16,512]{2,1,0:T(8,128)S(1)} custom-call(f32[8,16,512]{2,1,0:T(8,128)S(1)} %pad_maximum_fusion.1.x_ref, f32[640,128]{1,0:T(8,128)S(1)} %get-tuple-element.188.refs_0_, f32[640,128]{1,0:T(8,128)S(1)} %collective-permute-done.11.refs_1_, f32[640,128]{1,0:T(8,128)S(1)} %collective-permute-done.12.refs_2_, ...), custom_call_target="tpu_custom_call" | custom-call | tf_op jit(solution)/shard_map/cond/branch_1_fun/reduce_rows/pallas_call | solution.py:307
  (88 shorter events, 19.2 us)
Async XLA Ops:
  1.5 0.9 copy-start.1
  19.6 5.4 %copy-start.11 = (s32[32768]{0:T(1024)S(1)}, s32[32768]{0:T(1024)}, u32[]{:S(2)}) copy-start(s32[32768]{0:T(1024)} %param.8) | copy-start | bytes 393220
  19.6 54.0 %all-to-all-start.3 = ((f32[4,2048,128]{2,1,0:T(8,128)}), f32[4,2048,128]{2,1,0:T(8,128)}, u32[]{:S(2)}, u32[]{:S(2)}) async-start(f32[4,2048,128]{2,1,0:T(8,128)} %bitcast.82), calls=%async_computation.3 | async-start | bytes 8388608 | tf_op jit(solution)/shard_map/all_to_all | solution.py:389
  73.6 0.6 copy-start.9
  73.6 0.6 copy-start.12
  74.2 80.4 %all-to-all-start.2 = ((f32[4,2048,128]{2,1,0:T(8,128)}), f32[4,2048,128]{2,1,0:T(8,128)}, u32[]{:S(2)}, u32[]{:S(2)}) async-start(f32[4,2048,128]{2,1,0:T(8,128)} %get-tuple-element.145), calls=%async_computation.2 | async-start | bytes 8388608 | tf_op jit(solution)/shard_map/cond/branch_1_fun/all_to_all | solution.py:389
  90.6 1.5 copy-start
  93.3 74.0 %collective-permute-start.10 = (f32[4,640,128]{2,1,0:T(8,128)}, f32[4,640,128]{2,1,0:T(8,128)}, u32[]{:S(2)}, u32[]{:S(2)}) collective-permute-start(f32[4,640,128]{2,1,0:T(8,128)} %constant_dynamic-slice_fusion.11), channel_id=1, source_target_pairs={{0,16},{4,20},{8,24},{12,28},{16,0},{20,4},{24,8},{28,12},{1,17},{... | collective-permute-start | bytes 3932168 | tf_op jit(solution)/shard_map/cond/branch_1_fun/ppermute | solution.py:415
  167.3 57.7 %collective-permute-start.14 = (f32[4,640,128]{2,1,0:T(8,128)}, f32[4,640,128]{2,1,0:T(8,128)}, u32[]{:S(2)}, u32[]{:S(2)}) collective-permute-start(f32[4,640,128]{2,1,0:T(8,128)} %constant_dynamic-slice_fusion.10), channel_id=1, source_target_pairs={{0,16},{4,20},{8,24},{12,28},{16,0},{20,4},{24,8},{28,12},{1,17},{... | collective-permute-start | bytes 3932168 | tf_op jit(solution)/shard_map/cond/branch_1_fun/ppermute | solution.py:415
  169.1 58.4 %copy-start.2 = (f32[4,640,128]{2,1,0:T(8,128)}, f32[4,640,128]{2,1,0:T(8,128)S(1)}, u32[]{:S(2)}) copy-start(f32[4,640,128]{2,1,0:T(8,128)S(1)} %dynamic-slice_add_fusion.1) | copy-start | bytes 3932164 | tf_op jit(solution)/shard_map/cond
  169.1 79.9 %collective-permute-start.18 = (f32[2560,128]{1,0:T(8,128)S(1)}, f32[2560,128]{1,0:T(8,128)S(1)}, u32[]{:S(2)}, u32[]{:S(2)}) collective-permute-start(f32[2560,128]{1,0:T(8,128)S(1)} %bitcast.79), channel_id=1, source_target_pairs={{0,1},{1,0},{2,3},{3,2},{4,5},{5,4},{6,7},{7,6},{8,9},{9,8},{10,11... | collective-permute-start | bytes 3932168 | tf_op jit(solution)/shard_map/cond/branch_1_fun/ppermute | solution.py:223
  169.3 60.2 %collective-permute-start.11 = (f32[640,128]{1,0:T(8,128)S(1)}, f32[640,128]{1,0:T(8,128)S(1)}, u32[]{:S(2)}, u32[]{:S(2)}) collective-permute-start(f32[640,128]{1,0:T(8,128)S(1)} %get-tuple-element.187), channel_id=1, source_target_pairs={{0,4},{4,0},{8,12},{12,8},{16,20},{20,16},{24,28},{28,24},{1,5},{5... | collective-permute-start | bytes 983048 | tf_op jit(solution)/shard_map/cond/branch_1_fun/ppermute | solution.py:398
  227.5 46.2 %collective-permute-start.19 = (f32[2560,128]{1,0:T(8,128)}, f32[2560,128]{1,0:T(8,128)}, u32[]{:S(2)}, u32[]{:S(2)}) collective-permute-start(f32[2560,128]{1,0:T(8,128)} %bitcast.18), channel_id=1, source_target_pairs={{0,1},{1,0},{2,3},{3,2},{4,5},{5,4},{6,7},{7,6},{8,9},{9,8},{10,11... | collective-permute-start | bytes 3932168 | tf_op jit(solution)/shard_map/cond/branch_1_fun/ppermute | solution.py:223
  227.7 20.2 %collective-permute-start.20 = (f32[1280,128]{1,0:T(8,128)S(1)}, f32[1280,128]{1,0:T(8,128)S(1)}, u32[]{:S(2)}, u32[]{:S(2)}) collective-permute-start(f32[1280,128]{1,0:T(8,128)S(1)} %get-tuple-element.178), channel_id=1, source_target_pairs={{0,2},{1,3},{2,0},{3,1},{4,6},{5,7},{6,4},{7,5},{8,10},{9,11},{10,... | collective-permute-start | bytes 1966088 | tf_op jit(solution)/shard_map/cond/branch_1_fun/ppermute | solution.py:223
  229.5 10.5 %collective-permute-start.12 = (f32[640,128]{1,0:T(8,128)S(1)}, f32[640,128]{1,0:T(8,128)S(1)}, u32[]{:S(2)}, u32[]{:S(2)}) collective-permute-start(f32[640,128]{1,0:T(8,128)S(1)} %get-tuple-element.186), channel_id=1, source_target_pairs={{0,8},{4,12},{8,0},{12,4},{16,24},{20,28},{24,16},{28,20},{1,9},{5... | collective-permute-start | bytes 983048 | tf_op jit(solution)/shard_map/cond/branch_1_fun/ppermute | solution.py:398
  229.5 21.7 %copy-start.10 = (s32[4096]{0:T(1024)S(1)}, s32[4096]{0:T(1024)}, u32[]{:S(2)}) copy-start(s32[4096]{0:T(1024)} %copy-done.9) | copy-start | bytes 49156 | tf_op jit(solution)/shard_map/cond
  229.6 21.7 %copy-start.13 = (s32[4096]{0:T(1024)S(1)}, s32[4096]{0:T(1024)}, u32[]{:S(2)}) copy-start(s32[4096]{0:T(1024)} %copy-done.12) | copy-start | bytes 49156 | tf_op jit(solution)/shard_map/cond
  229.6 17.4 %collective-permute-start.13 = (f32[640,128]{1,0:T(8,128)S(1)}, f32[640,128]{1,0:T(8,128)S(1)}, u32[]{:S(2)}, u32[]{:S(2)}) collective-permute-start(f32[640,128]{1,0:T(8,128)S(1)} %get-tuple-element.185), channel_id=1, source_target_pairs={{0,12},{4,8},{8,4},{12,0},{16,28},{20,24},{24,20},{28,16},{1,13},{... | collective-permute-start | bytes 983048 | tf_op jit(solution)/shard_map/cond/branch_1_fun/ppermute | solution.py:398
  240.1 33.7 %collective-permute-start.22 = (f32[1280,128]{1,0:T(8,128)}, f32[1280,128]{1,0:T(8,128)}, u32[]{:S(2)}, u32[]{:S(2)}) collective-permute-start(f32[1280,128]{1,0:T(8,128)} %get-tuple-element.180), channel_id=1, source_target_pairs={{0,2},{1,3},{2,0},{3,1},{4,6},{5,7},{6,4},{7,5},{8,10},{9,11},{10,... | collective-permute-start | bytes 1966088 | tf_op jit(solution)/shard_map/cond/branch_1_fun/ppermute | solution.py:223
  246.9 9.2 %collective-permute-start.15 = (f32[640,128]{1,0:T(8,128)}, f32[640,128]{1,0:T(8,128)S(1)}, u32[]{:S(2)}, u32[]{:S(2)}) collective-permute-start(f32[640,128]{1,0:T(8,128)} %get-tuple-element.183), channel_id=1, source_target_pairs={{0,4},{4,0},{8,12},{12,8},{16,20},{20,16},{24,28},{28,24},{1,5},{5... | collective-permute-start | bytes 983048 | tf_op jit(solution)/shard_map/cond/branch_1_fun/ppermute | solution.py:398
  247.9 0.9 copy-start.7
  248.7 10.9 %collective-permute-start.16 = (f32[640,128]{1,0:T(8,128)}, f32[640,128]{1,0:T(8,128)S(1)}, u32[]{:S(2)}, u32[]{:S(2)}) collective-permute-start(f32[640,128]{1,0:T(8,128)} %get-tuple-element.182), channel_id=1, source_target_pairs={{0,8},{4,12},{8,0},{12,4},{16,24},{20,28},{24,16},{28,20},{1,9},{5... | collective-permute-start | bytes 983048 | tf_op jit(solution)/shard_map/cond/branch_1_fun/ppermute | solution.py:398
  249.0 2.3 copy-start.5
  249.0 16.2 %collective-permute-start.17 = (f32[640,128]{1,0:T(8,128)}, f32[640,128]{1,0:T(8,128)S(1)}, u32[]{:S(2)}, u32[]{:S(2)}) collective-permute-start(f32[640,128]{1,0:T(8,128)} %get-tuple-element.181), channel_id=1, source_target_pairs={{0,12},{4,8},{8,4},{12,0},{16,28},{20,24},{24,20},{28,16},{1,13},{... | collective-permute-start | bytes 983048 | tf_op jit(solution)/shard_map/cond/branch_1_fun/ppermute | solution.py:398
  256.1 28.5 %collective-permute-start.21 = (f32[1280,128]{1,0:T(8,128)}, f32[1280,128]{1,0:T(8,128)S(1)}, u32[]{:S(2)}, u32[]{:S(2)}) collective-permute-start(f32[1280,128]{1,0:T(8,128)} %copy-done.7), channel_id=1, source_target_pairs={{0,1},{1,0},{2,3},{3,2},{4,5},{5,4},{6,7},{7,6},{8,9},{9,8},{10,11... | collective-permute-start | bytes 1966088 | tf_op jit(solution)/shard_map/cond/branch_1_fun/ppermute | solution.py:223
  265.2 9.8 %copy-start.4 = (f32[1280,128]{1,0:T(8,128)S(1)}, f32[1280,128]{1,0:T(8,128)}, u32[]{:S(2)}) copy-start(f32[1280,128]{1,0:T(8,128)} %get-tuple-element.179) | copy-start | bytes 1966084 | tf_op jit(solution)/shard_map/cond
  273.8 3.1 %copy-start.8 = (f32[1280,128]{1,0:T(8,128)S(1)}, f32[1280,128]{1,0:T(8,128)}, u32[]{:S(2)}) copy-start(f32[1280,128]{1,0:T(8,128)} %copy-done.7) | copy-start | bytes 1966084 | tf_op jit(solution)/shard_map/cond
  273.8 9.0 %collective-permute-start.23 = (f32[1280,128]{1,0:T(8,128)}, f32[1280,128]{1,0:T(8,128)S(1)}, u32[]{:S(2)}, u32[]{:S(2)}) collective-permute-start(f32[1280,128]{1,0:T(8,128)} %collective-permute-done.22), channel_id=1, source_target_pairs={{0,1},{1,0},{2,3},{3,2},{4,5},{5,4},{6,7},{7,6},{8,9},{9,8},{10,11... | collective-permute-start | bytes 1966088 | tf_op jit(solution)/shard_map/cond/branch_1_fun/ppermute | solution.py:223
  276.8 4.6 %copy-start.3 = (f32[4,640,128]{2,1,0:T(8,128)S(1)}, f32[4,640,128]{2,1,0:T(8,128)}, u32[]{:S(2)}) copy-start(f32[4,640,128]{2,1,0:T(8,128)} %copy-done.2) | copy-start | bytes 3932164 | tf_op jit(solution)/shard_map/cond
  276.8 4.6 %copy-start.6 = (f32[2560,128]{1,0:T(8,128)S(1)}, f32[2560,128]{1,0:T(8,128)}, u32[]{:S(2)}) copy-start(f32[2560,128]{1,0:T(8,128)} %copy-done.5) | copy-start | bytes 3932164 | tf_op jit(solution)/shard_map/cond
  277.6 7.1 %collective-permute-start.24 = (f32[128,256]{1,0:T(8,128)S(1)}, f32[128,256]{1,0:T(8,128)S(1)}, u32[]{:S(2)}, u32[]{:S(2)}) collective-permute-start(f32[128,256]{1,0:T(8,128)S(1)} %fusion.24), channel_id=1, source_target_pairs={{0,2},{1,3},{2,0},{3,1},{4,6},{5,7},{6,4},{7,5},{8,10},{9,11},{10,... | collective-permute-start | bytes 393224 | tf_op jit(solution)/shard_map/cond/branch_1_fun/ppermute | solution.py:223

commit v3 on v2

--- a/solution.py
+++ b/solution.py
@@ -74,7 +74,8 @@
 def local_transform(panel, signs, devices, chunks, scale):
     rows, width = panel.shape
     outer = rows // INNER
-    steps_in = outer // 4
+    per_step = min(outer, 8)
+    steps_in = outer // per_step
     rows_out = 32
     steps_out = INNER // rows_out
     h = jnp.asarray(sylvester(INNER))
@@ -83,8 +84,8 @@
         grid=(steps_in + steps_out,),
         in_specs=[
             pl.BlockSpec((INNER, INNER), lambda t: (0, 0)),
-            pl.BlockSpec((4, 1, INNER), lambda t: (jnp.minimum(t, steps_in - 1), 0, 0)),
-            pl.BlockSpec((4, INNER, width), lambda t: (jnp.minimum(t, steps_in - 1), 0, 0)),
+            pl.BlockSpec((per_step, 1, INNER), lambda t: (jnp.minimum(t, steps_in - 1), 0, 0)),
+            pl.BlockSpec((per_step, INNER, width), lambda t: (jnp.minimum(t, steps_in - 1), 0, 0)),
         ],
         out_specs=[
             pl.BlockSpec(
@@ -180,6 +181,24 @@
     )(index.reshape(-1), sign.reshape(1), received)
 
 
+def add_kernel(a_ref, b_ref, *refs):
+    refs[-1][...] = a_ref[...] + b_ref[...]
+
+
+def add_blocks(a, b, after):
+    blocks, rows, width = a.shape
+    spec = pl.BlockSpec((1, rows, width), lambda t: (t, 0, 0))
+    return pl.pallas_call(
+        add_kernel,
+        grid=(blocks,),
+        in_specs=[spec, spec] + [pl.BlockSpec(memory_space=pl.ANY)] * len(after),
+        out_specs=spec,
+        out_shape=jax.ShapeDtypeStruct(a.shape, jnp.float32),
+        compiler_params=pltpu.CompilerParams(vmem_limit_bytes=VMEM_LIMIT),
+        name="add_blocks",
+    )(a, b, *after)
+
+
 def place_kernel(index_ref, *refs):
     *x_refs, out_ref, held = refs
     count = out_ref.shape[0]
@@ -377,7 +396,7 @@
     position = jnp.sum(jnp.where(my_onehot, my_ranks, 0), axis=0)
 
     mean = slots / devices
-    capacity = min(slots, -(-int(mean + 5.5 * math.sqrt(mean)) // 16) * 16)
+    capacity = min(slots, -(-int(mean + 4.2 * math.sqrt(mean)) // 16) * 16)
 
     def pick_index(owner, room):
         mine = owners == owner
@@ -412,7 +431,8 @@
             kept = lax.dynamic_slice_in_dim(picked, half * members, members)
             sent = lax.dynamic_slice_in_dim(picked, (1 - half) * members, members)
             partner = [(i, (i + members) % devices) for i in range(devices)]
-            whole = kept + lax.ppermute(sent, "row", partner)
+            came = lax.ppermute(sent, "row", partner)
+            whole = add_blocks(kept, came, [*arrived, *terms]) if k else kept + came
             new = gram_terms(whole.reshape(members * capacity, width))
             terms = new if terms is None else [a + b for a, b in zip(terms, new)]
             arrived += exchange_blocks(whole)

time: 304 us -> 289 us (0.951)
  waiting for transfers between devices: 150 us -> 125 us
  starting transfers between devices: 23.5 us -> 29.3 us
  matrix products: 9.67 us -> 13 us
    all_to_all x2, waiting for transfers between devices: 73.3 us -> 13.7 us  [within(): lax.all_to_all(value, 'row', split_axis=0, concat_axis=0, tiled=True, axi...]
    ppermute x2, waiting for transfers between devices: 53.9 us -> 70.5 us  [fast(): came = lax.ppermute(sent, 'row', partner)]
    ppermute x6, waiting for transfers between devices: 22.6 us -> 38.5 us  [exchange_blocks(): block = lax.ppermute(block, 'row', [(i, i ^ m) for i in range(devices)])]
    pallas_call x1, Pallas kernels: 17.2 us -> 13 us  [local_transform(): pl.pallas_call(functools.partial(transform_kernel, steps_in, outer, devic...]
    ppermute x2, starting transfers between devices: 2.77 us -> 6.14 us  [fast(): came = lax.ppermute(sent, 'row', partner)]
    dot_general x6, matrix products: 9.67 us -> 13 us  [dot(): lax.dot_general(a, b, (((0,), (0,)), ((), ())), precision=lax.Precision.H...]
  transfers between devices with their start and end apart: 17 -> 17, of which waited for: 8 -> 9; matrix products, arithmetic and copies ran while one was open for 18% -> 20% of each run, Pallas kernels for 10% -> 11%
where the time goes in v3:
time: 289 us; the launch traced here: 288 us
  waiting for transfers between devices  125 us (43%)
  Pallas kernels  63.8 us (22%)
  other arithmetic  37.2 us (13%)
  starting transfers between devices  29.3 us (10%)
  local copies, waits for them, and re-layouts  18 us (6%)
  matrix products  13 us (4%)
    ppermute x2, waiting for transfers between devices, fast(): came = lax.ppermute(sent, 'row', partner)  70.5 us
    ppermute x6, waiting for transfers between devices, exchange_blocks(): block = lax.ppermute(block, 'row', [(i, i ^ m) for i in range(devices)])  38.5 us
    reduce_sum x1, other arithmetic, pick_index(): jnp.sum(jnp.where(rank[:, None, :] == wanted, flat[:, None, :] + 8, 0), a...  23.6 us
    pallas_call x2, Pallas kernels, combine_and_pick(): pl.pallas_call(functools.partial(pick_kernel, steps_in), grid_spec=pltpu....  22.4 us
    pallas_call x1, Pallas kernels, reduce_rows(): pl.pallas_call(functools.partial(reduce_kernel, scale), in_specs=[pl.Bloc...  18.8 us
    all_to_all x2, waiting for transfers between devices, within(): lax.all_to_all(value, 'row', split_axis=0, concat_axis=0, tiled=True, axi...  13.7 us
    dot_general x6, matrix products, dot(): lax.dot_general(a, b, (((0,), (0,)), ((), ())), precision=lax.Precision.H...  13 us
    pallas_call x1, Pallas kernels, local_transform(): pl.pallas_call(functools.partial(transform_kernel, steps_in, outer, devic...  13 us
  transfers between devices with their start and end apart: 17, of which 9 were waited for; matrix products, arithmetic and copies ran while one was open for 20% of the time, Pallas kernels for 11%

profile of v3, /device:TPU:0, one launch (start us, length us, event | category | flops | bytes accessed | tf_op | source)
XLA Modules:
  0.0 287.5 jit_solution(10959487539320868510)
XLA Ops:
  2.4 13.0 %local_transform.1 = (f32[4,8,256,128]{3,2,1,0:T(8,128)}, f32[4,8,256,128]{3,2,1,0:T(8,128)}) custom-call(f32[256,256]{1,0:T(8,128)S(1)} %copy-done.8, f32[64,1,256]{2,1,0:T(1,128)S(1)} %bitcast.80, f32[64,256,128]{2,1,0:T(8,128)} %bitcast.86), custom_call_target="tpu_custom_call" | custom-call | flops 2147483648 | bytes 16777216 | tf_op jit(solution)/shard_map/local_transform/pallas_call | solution.py:82
  15.4 5.4 %all-to-all-start.3 = ((f32[4,2048,128]{2,1,0:T(8,128)}), f32[4,2048,128]{2,1,0:T(8,128)}, u32[]{:S(2)}, u32[]{:S(2)}) async-start(f32[4,2048,128]{2,1,0:T(8,128)} %bitcast.82), calls=%async_computation.3 | async-start | bytes 8388608 | tf_op jit(solution)/shard_map/all_to_all | solution.py:408
  21.0 2.3 reduce-window.30
  23.9 2.3 reduce-window.34
  27.0 2.3 reduce-window.26
  32.0 23.6 %select_reduce_fusion.1 = (s32[8,608]{1,0:T(8,128)S(1)}, s32[8,608]{1,0:T(8,128)S(1)}) fusion(s32[8,4096]{1,0:T(8,128)S(1)} %bitcast_select_fusion.1, s32[8,4096]{1,0:T(8,128)S(1)} %get-tuple-element.209, s32[8,4096]{1,0:T(8,128)S(1)} %get-tuple-element.213), kind=kLoop, calls=%fused_computation.164 | loop fusion | flops 119527936 | bytes 432128 | tf_op jit(solution)/shard_map/reduce_sum | solution.py:405
  55.6 13.7 %all-to-all-done.3 = f32[4,2048,128]{2,1,0:T(8,128)} async-done(((f32[4,2048,128]{2,1,0:T(8,128)}), f32[4,2048,128]{2,1,0:T(8,128)}, u32[]{:S(2)}, u32[]{:S(2)}) %all-to-all-start.3) | async-done | bytes 4194336 | tf_op jit(solution)/shard_map/all_to_all | solution.py:408
  69.3 216.5 %conditional.1 = (f32[4096,128]{1,0:T(8,128)}, f32[128,512]{1,0:T(8,128)}) conditional(s32[]{:T(128)} %convert_element_type.23, (s32[4096]{0:T(1024)S(1)}, s32[4096]{0:T(1024)S(1)}, s32[]{:T(128)}, s32[8,4096]{1,0:T(8,128)S(1)}, s32[8,4096]{1,0:T(8,128)S(1)}, /*index=5*/s32[8,4096]{1,0:T(8,128)S(1)}, s32[8,4096]{1,0:T(8,128)S(1)}, ...), branch_computations={%region_11.15_spmd, %region_15.16_spmd} | conditional | flops 2040946688 | bytes 273070144 | solution.py:459
  70.0 4.8 %all-to-all-start.2 = ((f32[4,2048,128]{2,1,0:T(8,128)}), f32[4,2048,128]{2,1,0:T(8,128)}, u32[]{:S(2)}, u32[]{:S(2)}) async-start(f32[4,2048,128]{2,1,0:T(8,128)} %get-tuple-element.145), calls=%async_computation.2 | async-start | bytes 8388608 | tf_op jit(solution)/shard_map/cond/branch_1_fun/all_to_all | solution.py:408
  74.9 11.2 %combine_and_pick.2 = f32[8,608,128]{2,1,0:T(8,128)S(1)} custom-call(s32[4864]{0:T(1024)S(1)} %reshape.347.index_ref, s32[1]{0:T(128)} %bitcast.8.sign_ref, f32[4,2048,128]{2,1,0:T(8,128)} %get-tuple-element.143.x_ref), custom_call_target="tpu_custom_call" | custom-call | flops 16777216 | bytes 33554432 | tf_op jit(solution)/shard_map/cond/branch_1_fun/combine_and_pick/pallas_call | solution.py:158
  87.3 2.8 collective-permute-start.10
  90.0 56.4 %collective-permute-done.10 = f32[4,608,128]{2,1,0:T(8,128)} collective-permute-done((f32[4,608,128]{2,1,0:T(8,128)}, f32[4,608,128]{2,1,0:T(8,128)}, u32[]{:S(2)}, u32[]{:S(2)}) %collective-permute-start.10) | collective-permute-done | bytes 1245216 | tf_op jit(solution)/shard_map/cond/branch_1_fun/ppermute | solution.py:434
  146.4 2.5 dynamic-slice_add_fusion
  148.9 2.2 constant_dynamic-slice_fusion.8
  152.6 11.2 %combine_and_pick.3 = f32[8,608,128]{2,1,0:T(8,128)S(1)} custom-call(s32[4864]{0:T(1024)S(1)} %reshape.349.index_ref, s32[1]{0:T(128)} %bitcast.8.sign_ref, f32[4,2048,128]{2,1,0:T(8,128)} %all-to-all-done.2.x_ref), custom_call_target="tpu_custom_call" | custom-call | flops 16777216 | bytes 33554432 | tf_op jit(solution)/shard_map/cond/branch_1_fun/combine_and_pick/pallas_call | solution.py:158
  165.1 3.4 %collective-permute-start.14 = (f32[4,608,128]{2,1,0:T(8,128)}, f32[4,608,128]{2,1,0:T(8,128)S(1)}, u32[]{:S(2)}, u32[]{:S(2)}) collective-permute-start(f32[4,608,128]{2,1,0:T(8,128)} %get-tuple-element.177), channel_id=1, source_target_pairs={{0,16},{4,20},{8,24},{12,28},{16,0},{20,4},{24,8},{28,12},{1,17},{... | collective-permute-start | bytes 3735560 | tf_op jit(solution)/shard_map/cond/branch_1_fun/ppermute | solution.py:434
  169.9 1.8 collective-permute-start.11
  171.7 3.5 %collective-permute-start.12 = (f32[608,128]{1,0:T(8,128)S(1)}, f32[608,128]{1,0:T(8,128)S(1)}, u32[]{:S(2)}, u32[]{:S(2)}) collective-permute-start(f32[608,128]{1,0:T(8,128)S(1)} %get-tuple-element.188), channel_id=1, source_target_pairs={{0,8},{4,12},{8,0},{12,4},{16,24},{20,28},{24,16},{28,20},{1,9},{5... | collective-permute-start | bytes 933896 | tf_op jit(solution)/shard_map/cond/branch_1_fun/ppermute | solution.py:417
  177.0 2.0 fusion.12.refs_6_
  179.0 1.8 fusion.8.refs_5_
  180.8 3.2 %fusion.refs_4_ = f32[128,256]{1,0:T(8,128)S(1)} fusion(f32[2432,128]{1,0:T(8,128)} %bitcast.13, f32[2432,128]{1,0:T(8,128)} %collective-permute-done.15), kind=kOutput, calls=%fused_computation.2 | convolution fusion | flops 478773248 | bytes 2621440 | tf_op jit(solution)/shard_map/cond/branch_1_fun/dot_general | solution.py:250
  184.0 19.1 %collective-permute-done.12.refs_2_ = f32[608,128]{1,0:T(8,128)S(1)} collective-permute-done((f32[608,128]{1,0:T(8,128)S(1)}, f32[608,128]{1,0:T(8,128)S(1)}, u32[]{:S(2)}, u32[]{:S(2)}) %collective-permute-start.12) | collective-permute-done | bytes 311328 | tf_op jit(solution)/shard_map/cond/branch_1_fun/ppermute | solution.py:417
  203.1 6.0 %collective-permute-done.13.refs_3_ = f32[608,128]{1,0:T(8,128)S(1)} collective-permute-done((f32[608,128]{1,0:T(8,128)S(1)}, f32[608,128]{1,0:T(8,128)S(1)}, u32[]{:S(2)}, u32[]{:S(2)}) %collective-permute-start.13) | collective-permute-done | bytes 311328 | tf_op jit(solution)/shard_map/cond/branch_1_fun/ppermute | solution.py:417
  209.1 14.0 %collective-permute-done.14.b_ref = f32[4,608,128]{2,1,0:T(8,128)S(1)} collective-permute-done((f32[4,608,128]{2,1,0:T(8,128)}, f32[4,608,128]{2,1,0:T(8,128)S(1)}, u32[]{:S(2)}, u32[]{:S(2)}) %collective-permute-start.14) | collective-permute-done | bytes 1245216 | tf_op jit(solution)/shard_map/cond/branch_1_fun/ppermute | solution.py:434
  233.2 5.5 %collective-permute-done.18.refs_5_ = f32[608,128]{1,0:T(8,128)S(1)} collective-permute-done((f32[608,128]{1,0:T(8,128)}, f32[608,128]{1,0:T(8,128)S(1)}, u32[]{:S(2)}, u32[]{:S(2)}) %collective-permute-start.18) | collective-permute-done | bytes 311328 | tf_op jit(solution)/shard_map/cond/branch_1_fun/ppermute | solution.py:417
  238.7 2.5 collective-permute-done.19.refs_6_
  241.1 5.5 %collective-permute-done.20.refs_7_ = f32[608,128]{1,0:T(8,128)} collective-permute-done((f32[608,128]{1,0:T(8,128)}, f32[608,128]{1,0:T(8,128)}, u32[]{:S(2)}, u32[]{:S(2)}) %collective-permute-start.20) | collective-permute-done | bytes 311328 | tf_op jit(solution)/shard_map/cond/branch_1_fun/ppermute | solution.py:417
  246.6 9.4 %place_rows.1 = f32[4096,128]{1,0:T(8,128)} custom-call(s32[4096]{0:T(1024)S(1)} %fusion.39.index_ref, f32[608,128]{1,0:T(8,128)S(1)} %get-tuple-element.190.refs_0_, f32[608,128]{1,0:T(8,128)S(1)} %collective-permute-done.11.refs_1_, f32[608,128]{1,0:T(8,128)S(1)} %collective-permute-done.12.refs_2_, f32[608,128]{1,0:T(8,128)S(1)} %copy-done.1, ...), custom_call_target="tpu_custom_call" | custom-call | tf_op jit(solution)/shard_map/cond/branch_1_fun/place_rows/pallas_call | solution.py:225
  257.2 1.8 fusion.24
  260.5 2.5 fusion.33
  263.0 1.9 collective-permute-done.24
  267.1 18.8 %reduce_rows.1 = f32[8,16,512]{2,1,0:T(8,128)} custom-call(f32[8,16,512]{2,1,0:T(8,128)S(1)} %pad_maximum_fusion.1.x_ref, f32[608,128]{1,0:T(8,128)S(1)} %get-tuple-element.190.refs_0_, f32[608,128]{1,0:T(8,128)S(1)} %collective-permute-done.11.refs_1_, f32[608,128]{1,0:T(8,128)S(1)} %collective-permute-done.12.refs_2_, f32[608,128]{1,0:T(8,128)S(1)} %copy-done.1, ...), custom_call_target="tpu_custom_call" | custom-call | tf_op jit(solution)/shard_map/cond/branch_1_fun/reduce_rows/pallas_call | solution.py:326
  (88 shorter events, 29.7 us)
Async XLA Ops:
  1.5 0.9 copy-start.8
  15.4 5.4 %copy-start.12 = (s32[32768]{0:T(1024)S(1)}, s32[32768]{0:T(1024)}, u32[]{:S(2)}) copy-start(s32[32768]{0:T(1024)} %param.8) | copy-start | bytes 393220
  15.4 54.0 %all-to-all-start.3 = ((f32[4,2048,128]{2,1,0:T(8,128)}), f32[4,2048,128]{2,1,0:T(8,128)}, u32[]{:S(2)}, u32[]{:S(2)}) async-start(f32[4,2048,128]{2,1,0:T(8,128)} %bitcast.82), calls=%async_computation.3 | async-start | bytes 8388608 | tf_op jit(solution)/shard_map/all_to_all | solution.py:408
  69.3 0.6 copy-start.11
  69.3 0.6 copy-start.13
  70.0 82.7 %all-to-all-start.2 = ((f32[4,2048,128]{2,1,0:T(8,128)}), f32[4,2048,128]{2,1,0:T(8,128)}, u32[]{:S(2)}, u32[]{:S(2)}) async-start(f32[4,2048,128]{2,1,0:T(8,128)} %get-tuple-element.145), calls=%async_computation.2 | async-start | bytes 8388608 | tf_op jit(solution)/shard_map/cond/branch_1_fun/all_to_all | solution.py:408
  87.3 59.2 %collective-permute-start.10 = (f32[4,608,128]{2,1,0:T(8,128)}, f32[4,608,128]{2,1,0:T(8,128)}, u32[]{:S(2)}, u32[]{:S(2)}) collective-permute-start(f32[4,608,128]{2,1,0:T(8,128)} %constant_dynamic-slice_fusion.12), channel_id=1, source_target_pairs={{0,16},{4,20},{8,24},{12,28},{16,0},{20,4},{24,8},{28,12},{1,17},{... | collective-permute-start | bytes 3735560 | tf_op jit(solution)/shard_map/cond/branch_1_fun/ppermute | solution.py:434
  148.9 26.3 %collective-permute-start.15 = (f32[2432,128]{1,0:T(8,128)}, f32[2432,128]{1,0:T(8,128)}, u32[]{:S(2)}, u32[]{:S(2)}) collective-permute-start(f32[2432,128]{1,0:T(8,128)} %bitcast.13), channel_id=1, source_target_pairs={{0,1},{1,0},{2,3},{3,2},{4,5},{5,4},{6,7},{7,6},{8,9},{9,8},{10,11... | collective-permute-start | bytes 3735560 | tf_op jit(solution)/shard_map/cond/branch_1_fun/ppermute | solution.py:242
  151.1 17.4 %collective-permute-start.16 = (f32[1216,128]{1,0:T(8,128)S(1)}, f32[1216,128]{1,0:T(8,128)}, u32[]{:S(2)}, u32[]{:S(2)}) collective-permute-start(f32[1216,128]{1,0:T(8,128)S(1)} %get-tuple-element.185), channel_id=1, source_target_pairs={{0,2},{1,3},{2,0},{3,1},{4,6},{5,7},{6,4},{7,5},{8,10},{9,11},{10,... | collective-permute-start | bytes 1867784 | tf_op jit(solution)/shard_map/cond/branch_1_fun/ppermute | solution.py:242
  165.1 58.0 %collective-permute-start.14 = (f32[4,608,128]{2,1,0:T(8,128)}, f32[4,608,128]{2,1,0:T(8,128)S(1)}, u32[]{:S(2)}, u32[]{:S(2)}) collective-permute-start(f32[4,608,128]{2,1,0:T(8,128)} %get-tuple-element.177), channel_id=1, source_target_pairs={{0,16},{4,20},{8,24},{12,28},{16,0},{20,4},{24,8},{28,12},{1,17},{... | collective-permute-start | bytes 3735560 | tf_op jit(solution)/shard_map/cond/branch_1_fun/ppermute | solution.py:434
  168.5 10.5 %copy-start.10 = (f32[1216,128]{1,0:T(8,128)S(1)}, f32[1216,128]{1,0:T(8,128)}, u32[]{:S(2)}) copy-start(f32[1216,128]{1,0:T(8,128)} %get-tuple-element.186) | copy-start | bytes 1867780 | tf_op jit(solution)/shard_map/cond
  168.5 10.5 %collective-permute-start.17 = (f32[1216,128]{1,0:T(8,128)}, f32[1216,128]{1,0:T(8,128)S(1)}, u32[]{:S(2)}, u32[]{:S(2)}) collective-permute-start(f32[1216,128]{1,0:T(8,128)} %collective-permute-done.16), channel_id=1, source_target_pairs={{0,1},{1,0},{2,3},{3,2},{4,5},{5,4},{6,7},{7,6},{8,9},{9,8},{10,11... | collective-permute-start | bytes 1867784 | tf_op jit(solution)/shard_map/cond/branch_1_fun/ppermute | solution.py:242
  169.9 14.1 %collective-permute-start.11 = (f32[608,128]{1,0:T(8,128)S(1)}, f32[608,128]{1,0:T(8,128)S(1)}, u32[]{:S(2)}, u32[]{:S(2)}) collective-permute-start(f32[608,128]{1,0:T(8,128)S(1)} %get-tuple-element.189), channel_id=1, source_target_pairs={{0,4},{4,0},{8,12},{12,8},{16,20},{20,16},{24,28},{28,24},{1,5},{5... | collective-permute-start | bytes 933896 | tf_op jit(solution)/shard_map/cond/branch_1_fun/ppermute | solution.py:417
  171.7 31.5 %collective-permute-start.12 = (f32[608,128]{1,0:T(8,128)S(1)}, f32[608,128]{1,0:T(8,128)S(1)}, u32[]{:S(2)}, u32[]{:S(2)}) collective-permute-start(f32[608,128]{1,0:T(8,128)S(1)} %get-tuple-element.188), channel_id=1, source_target_pairs={{0,8},{4,12},{8,0},{12,4},{16,24},{20,28},{24,16},{28,20},{1,9},{5... | collective-permute-start | bytes 933896 | tf_op jit(solution)/shard_map/cond/branch_1_fun/ppermute | solution.py:417
  175.2 33.9 %collective-permute-start.13 = (f32[608,128]{1,0:T(8,128)S(1)}, f32[608,128]{1,0:T(8,128)S(1)}, u32[]{:S(2)}, u32[]{:S(2)}) collective-permute-start(f32[608,128]{1,0:T(8,128)S(1)} %get-tuple-element.187), channel_id=1, source_target_pairs={{0,12},{4,8},{8,4},{12,0},{16,28},{20,24},{24,20},{28,16},{1,13},{... | collective-permute-start | bytes 933896 | tf_op jit(solution)/shard_map/cond/branch_1_fun/ppermute | solution.py:417
  178.9 46.7 %copy-start.4 = (f32[128,256]{1,0:T(8,128)}, f32[128,256]{1,0:T(8,128)S(1)}, u32[]{:S(2)}) copy-start(f32[128,256]{1,0:T(8,128)S(1)} %fusion.12.refs_6_) | copy-start | bytes 393220 | tf_op jit(solution)/shard_map/cond
  209.1 16.6 %copy-start = (f32[608,128]{1,0:T(8,128)}, f32[608,128]{1,0:T(8,128)S(1)}, u32[]{:S(2)}) copy-start(f32[608,128]{1,0:T(8,128)S(1)} %collective-permute-done.13.refs_3_) | copy-start | bytes 933892 | tf_op jit(solution)/shard_map/cond
  223.1 1.0 copy-start.2
  224.2 1.3 copy-start.3
  225.7 0.7 copy-start.6
  226.3 20.3 %copy-start.1 = (f32[608,128]{1,0:T(8,128)S(1)}, f32[608,128]{1,0:T(8,128)}, u32[]{:S(2)}) copy-start(f32[608,128]{1,0:T(8,128)} %copy-done) | copy-start | bytes 933892 | tf_op jit(solution)/shard_map/cond
  226.3 29.7 %collective-permute-start.21 = (f32[2432,128]{1,0:T(8,128)S(1)}, f32[2432,128]{1,0:T(8,128)}, u32[]{:S(2)}, u32[]{:S(2)}) collective-permute-start(f32[2432,128]{1,0:T(8,128)S(1)} %bitcast.77), channel_id=1, source_target_pairs={{0,1},{1,0},{2,3},{3,2},{4,5},{5,4},{6,7},{7,6},{8,9},{9,8},{10,11... | collective-permute-start | bytes 3735560 | tf_op jit(solution)/shard_map/cond/branch_1_fun/ppermute | solution.py:242
  227.4 28.6 %collective-permute-start.22 = (f32[1216,128]{1,0:T(8,128)}, f32[1216,128]{1,0:T(8,128)}, u32[]{:S(2)}, u32[]{:S(2)}) collective-permute-start(f32[1216,128]{1,0:T(8,128)} %get-tuple-element.180), channel_id=1, source_target_pairs={{0,2},{1,3},{2,0},{3,1},{4,6},{5,7},{6,4},{7,5},{8,10},{9,11},{10,... | collective-permute-start | bytes 1867784 | tf_op jit(solution)/shard_map/cond/branch_1_fun/ppermute | solution.py:242
  228.9 9.7 %collective-permute-start.18 = (f32[608,128]{1,0:T(8,128)}, f32[608,128]{1,0:T(8,128)S(1)}, u32[]{:S(2)}, u32[]{:S(2)}) collective-permute-start(f32[608,128]{1,0:T(8,128)} %get-tuple-element.183), channel_id=1, source_target_pairs={{0,4},{4,0},{8,12},{12,8},{16,20},{20,16},{24,28},{28,24},{1,5},{5... | collective-permute-start | bytes 933896 | tf_op jit(solution)/shard_map/cond/branch_1_fun/ppermute | solution.py:417
  230.7 10.4 %collective-permute-start.19 = (f32[608,128]{1,0:T(8,128)}, f32[608,128]{1,0:T(8,128)S(1)}, u32[]{:S(2)}, u32[]{:S(2)}) collective-permute-start(f32[608,128]{1,0:T(8,128)} %get-tuple-element.182), channel_id=1, source_target_pairs={{0,8},{4,12},{8,0},{12,4},{16,24},{20,28},{24,16},{28,20},{1,9},{5... | collective-permute-start | bytes 933896 | tf_op jit(solution)/shard_map/cond/branch_1_fun/ppermute | solution.py:417
  231.4 15.2 %collective-permute-start.20 = (f32[608,128]{1,0:T(8,128)}, f32[608,128]{1,0:T(8,128)}, u32[]{:S(2)}, u32[]{:S(2)}) collective-permute-start(f32[608,128]{1,0:T(8,128)} %get-tuple-element.181), channel_id=1, source_target_pairs={{0,12},{4,8},{8,4},{12,0},{16,28},{20,24},{24,20},{28,16},{1,13},{... | collective-permute-start | bytes 933896 | tf_op jit(solution)/shard_map/cond/branch_1_fun/ppermute | solution.py:417
  246.6 10.6 %copy-start.5 = (f32[128,256]{1,0:T(8,128)S(1)}, f32[128,256]{1,0:T(8,128)}, u32[]{:S(2)}) copy-start(f32[128,256]{1,0:T(8,128)} %copy-done.4) | copy-start | bytes 393220 | tf_op jit(solution)/shard_map/cond
  246.6 10.6 %copy-start.9 = (f32[1216,128]{1,0:T(8,128)S(1)}, f32[1216,128]{1,0:T(8,128)}, u32[]{:S(2)}) copy-start(f32[1216,128]{1,0:T(8,128)} %get-tuple-element.179) | copy-start | bytes 1867780 | tf_op jit(solution)/shard_map/cond
  256.0 4.5 %copy-start.7 = (f32[128,256]{1,0:T(8,128)S(1)}, f32[128,256]{1,0:T(8,128)}, u32[]{:S(2)}) copy-start(f32[128,256]{1,0:T(8,128)} %copy-done.6) | copy-start | bytes 393220 | tf_op jit(solution)/shard_map/cond
  256.0 7.0 %collective-permute-start.23 = (f32[1216,128]{1,0:T(8,128)}, f32[1216,128]{1,0:T(8,128)S(1)}, u32[]{:S(2)}, u32[]{:S(2)}) collective-permute-start(f32[1216,128]{1,0:T(8,128)} %collective-permute-done.22), channel_id=1, source_target_pairs={{0,1},{1,0},{2,3},{3,2},{4,5},{5,4},{6,7},{7,6},{8,9},{9,8},{10,11... | collective-permute-start | bytes 1867784 | tf_op jit(solution)/shard_map/cond/branch_1_fun/ppermute | solution.py:242
  259.0 5.9 %collective-permute-start.24 = (f32[128,256]{1,0:T(8,128)S(1)}, f32[128,256]{1,0:T(8,128)S(1)}, u32[]{:S(2)}, u32[]{:S(2)}) collective-permute-start(f32[128,256]{1,0:T(8,128)S(1)} %fusion.24), channel_id=1, source_target_pairs={{0,2},{1,3},{2,0},{3,1},{4,6},{5,7},{6,4},{7,5},{8,10},{9,11},{10,... | collective-permute-start | bytes 393224 | tf_op jit(solution)/shard_map/cond/branch_1_fun/ppermute | solution.py:242
